TPU v7x, 128 devices: a whole 4x4x4 slice. The times are simulated.
128 devices in a mesh: pipe: 2 (over x_lo), dp: 64 (over z, y, x_hi, core).
Axes of the slice: x: 4 (x_hi: 2, x_lo: 2; x = x_hi * 2 + x_lo), y: 4, z: 4, core: 2. Of those that a mesh axis runs over, the one named last changes fastest.
Arguments:
- stack_input: bfloat16 [2, 8192, 8192], P(None, 'dp', 'pipe'), may hold values from -6 to 6
- output_gradient: bfloat16 [2, 8192, 8192], P(None, 'dp', 'pipe'), may hold values from -1.5 to 1.5
- norm_scale_weight: float32 [2, 8192], P('pipe'), may hold values from 0.5 to 1.5
- row_adapter_index: int32 [2, 8192, 1], P(None, 'dp'), may hold values from 0 to 63; in each aligned block of 128 rows (0 to 127, 128 to 255, ..., all dimensions but the last counted through in order) at most 4 rows name the same one
- adapter_owner_index: int32 [64], replicated, may hold values from 0 to 63, each once
- adapter_down_weight: bfloat16 [2, 64, 32, 8192], P('pipe', 'dp'), may hold values from -0.0625 to 0.0625
- adapter_up_weight: bfloat16 [2, 64, 32, 8192], P('pipe', 'dp'), may hold values from -1 to 1
- down_first_moment: float32 [2, 64, 32, 8192], P('pipe', 'dp'), may hold values from -12 to 12
- down_second_moment: float32 [2, 64, 32, 8192], P('pipe', 'dp'), may hold values from 1 to 1000
- up_first_moment: float32 [2, 64, 32, 8192], P('pipe', 'dp'), may hold values from -1.2 to 1.2
- up_second_moment: float32 [2, 64, 32, 8192], P('pipe', 'dp'), may hold values from 0.01 to 10
Outputs:
- down_weight_next: bfloat16 [2, 64, 32, 8192], P('pipe', 'dp')
- up_weight_next: bfloat16 [2, 64, 32, 8192], P('pipe', 'dp')
- down_first_moment_next: float32 [2, 64, 32, 8192], P('pipe', 'dp')
- down_second_moment_next: float32 [2, 64, 32, 8192], P('pipe', 'dp')
- up_first_moment_next: float32 [2, 64, 32, 8192], P('pipe', 'dp')
- up_second_moment_next: float32 [2, 64, 32, 8192], P('pipe', 'dp')
Inputs may be any that keep to these rules, and one draw needn't show every extreme that they name: `row_adapter_index`: in each micro-batch the 128 rows of one device name any one adapter at most 4 times. Every index of dp owns exactly one adapter; adapter a's projections and moments stand at index adapter_owner_index[a] of their second dimension.
All inputs are finite; a program needn't handle non-finite values.
Results may differ from a plain program's by a relative error of at most 0.0055.
Values may be sent and summed in bfloat16 or wider, within the bound.
A program may use at most 192 MiB of HBM per device.

v0:
```python
import jax
import jax.numpy as jnp
from jax import lax
from jax.sharding import PartitionSpec as P

adapter_scale = 0.5
beta_one = 0.9
beta_two = 0.999
step_count = 10
learn_rate = 0.001
decay_rate = 0.01
eps_root = 1e-08
eps_norm = 1e-05


def from_behind(array, axis, by):
    count = lax.axis_size(axis)
    pairs = [(i, i + by) for i in range(count) if 0 <= i + by < count]
    return lax.ppermute(array, axis, pairs)


def route_table(row_adapter_index, adapter_owner_index, slot_count, capacity):
    labels = row_adapter_index[..., 0]
    adapter_count = adapter_owner_index.shape[0]
    matches = (labels[..., None] == jnp.arange(adapter_count, dtype=jnp.int32)).astype(jnp.int32)
    target = jnp.sum(matches * adapter_owner_index, axis=-1)
    row_count = labels.shape[-1]
    alike = (target[..., :, None] == target[..., None, :]).astype(jnp.int32)
    earlier = (
        jnp.arange(row_count, dtype=jnp.int32)[None, :]
        < jnp.arange(row_count, dtype=jnp.int32)[:, None]
    ).astype(jnp.int32)
    within = jnp.sum(alike * earlier, axis=-1)
    slot_flat = target * capacity + within
    return (
        slot_flat[..., None, :] == jnp.arange(slot_count * capacity, dtype=jnp.int32)[:, None]
    ).astype(jnp.bfloat16)


def normalize(hidden_state, gain_row):
    value_entries = hidden_state.astype(jnp.float32)
    factor = lax.rsqrt(jnp.mean(value_entries * value_entries, axis=-1, keepdims=True) + eps_norm)
    return (value_entries, factor, (value_entries * factor * gain_row).astype(jnp.bfloat16))


def keep_at(storage, element, slot_at, active):
    previous = lax.dynamic_index_in_dim(storage, slot_at, 0, keepdims=False)
    return lax.dynamic_update_index_in_dim(
        storage, jnp.where(active, element, previous), slot_at, 0
    )


def adamw_update(weight_in, moment_one, moment_two, gradient):
    first_new = beta_one * moment_one + (1.0 - beta_one) * gradient
    second_new = beta_two * moment_two + (1.0 - beta_two) * gradient * gradient
    first_hat = first_new / (1.0 - beta_one**step_count)
    second_hat = second_new / (1.0 - beta_two**step_count)
    value_entries = weight_in.astype(jnp.float32)
    result = value_entries - learn_rate * (
        first_hat / jnp.sqrt(second_hat + eps_root) + decay_rate * value_entries
    )
    return (result.astype(jnp.bfloat16), first_new, second_new)


def body(
    stack_input,
    output_gradient,
    norm_scale_weight,
    row_adapter_index,
    adapter_owner_index,
    adapter_down_weight,
    adapter_up_weight,
    down_first_moment,
    down_second_moment,
    up_first_moment,
    up_second_moment,
):
    section_count = lax.axis_size("pipe")
    slot_count = lax.axis_size("dp")
    section_index = lax.axis_index("pipe")
    micro_count = stack_input.shape[0]
    capacity = max(2, 2 * stack_input.shape[1] // slot_count)
    placing = route_table(row_adapter_index, adapter_owner_index, slot_count, capacity)
    sent_input = jnp.einsum(
        "bqt,btf->bqf", placing, stack_input, preferred_element_type=jnp.float32
    ).astype(jnp.bfloat16)
    sent_grad = jnp.einsum(
        "bqt,btf->bqf", placing, output_gradient, preferred_element_type=jnp.float32
    ).astype(jnp.bfloat16)
    piece_shape = (micro_count, slot_count, capacity, stack_input.shape[2])
    got_input, got_grad = (
        lax.all_to_all(
            sent_input.reshape(piece_shape), "dp", split_axis=1, concat_axis=1, tiled=True
        ),
        lax.all_to_all(
            sent_grad.reshape(piece_shape), "dp", split_axis=1, concat_axis=1, tiled=True
        ),
    )
    full_input, full_grad = (
        lax.all_gather(got_input, "pipe", axis=3, tiled=True),
        lax.all_gather(got_grad, "pipe", axis=3, tiled=True),
    )
    rows_total = slot_count * capacity
    features = full_input.shape[3]
    full_input = full_input.reshape(micro_count, rows_total, features)
    full_grad = full_grad.reshape(micro_count, rows_total, features)
    gain_row = norm_scale_weight[0]
    down_weight = adapter_down_weight[0, 0]
    up_weight = adapter_up_weight[0, 0]
    rank_width = down_weight.shape[0]
    tick_count = micro_count + section_count - 1
    carried = jnp.zeros((rows_total, features), jnp.bfloat16)
    kept_hidden = jnp.zeros((micro_count, rows_total, features), jnp.bfloat16)
    for moment in range(tick_count):
        position = moment - section_index
        active = (position >= 0) & (position < micro_count)
        slot_at = jnp.clip(position, 0, micro_count - 1)
        hidden_state = jnp.where(
            section_index == 0, full_input[min(moment, micro_count - 1)], carried
        )
        value_entries, factor, norm_output = normalize(hidden_state, gain_row)
        rank_projection = jnp.einsum(
            "sd,rd->sr", norm_output, down_weight, preferred_element_type=jnp.float32
        ).astype(jnp.bfloat16)
        advanced = (
            value_entries
            + adapter_scale
            * jnp.dot(rank_projection, up_weight, preferred_element_type=jnp.float32)
        ).astype(jnp.bfloat16)
        kept_hidden = keep_at(kept_hidden, hidden_state, slot_at, active)
        if moment < tick_count - 1:
            carried = from_behind(advanced, "pipe", 1)
    carried = jnp.zeros((rows_total, features), jnp.bfloat16)
    down_gradient = jnp.zeros((rank_width, features), jnp.float32)
    up_gradient = jnp.zeros((rank_width, features), jnp.float32)
    for moment in range(tick_count):
        position = moment - (section_count - 1 - section_index)
        active = (position >= 0) & (position < micro_count)
        current_weight = active.astype(jnp.float32)
        slot_at = jnp.clip(position, 0, micro_count - 1)
        arriving_input = jnp.where(
            section_index == section_count - 1, full_grad[min(moment, micro_count - 1)], carried
        )
        hidden_state = lax.dynamic_index_in_dim(kept_hidden, slot_at, 0, keepdims=False)
        value_entries = hidden_state.astype(jnp.float32)
        factor = lax.rsqrt(
            jnp.mean(value_entries * value_entries, axis=-1, keepdims=True) + eps_norm
        )
        norm_output = (value_entries * factor * gain_row).astype(jnp.bfloat16)
        rank_projection = jnp.einsum(
            "sd,rd->sr", norm_output, down_weight, preferred_element_type=jnp.float32
        ).astype(jnp.bfloat16)
        rank_projection_gradient = (
            adapter_scale
            * jnp.einsum("sd,rd->sr", arriving_input, up_weight, preferred_element_type=jnp.float32)
        ).astype(jnp.bfloat16)
        up_gradient = up_gradient + current_weight * adapter_scale * jnp.einsum(
            "sr,sd->rd", rank_projection, arriving_input, preferred_element_type=jnp.float32
        )
        down_gradient = down_gradient + current_weight * jnp.einsum(
            "sr,sd->rd", rank_projection_gradient, norm_output, preferred_element_type=jnp.float32
        )
        if moment < tick_count - 1:
            norm_output_gradient = jnp.dot(
                rank_projection_gradient, down_weight, preferred_element_type=jnp.float32
            )
            scaled = gain_row * norm_output_gradient
            returned = (
                arriving_input.astype(jnp.float32)
                + factor * scaled
                - value_entries
                * factor**3
                * jnp.mean(scaled * value_entries, axis=-1, keepdims=True)
            )
            carried = from_behind(returned.astype(jnp.bfloat16), "pipe", -1)
    down_weight_next, down_first_moment_next, down_second_moment_next = adamw_update(
        adapter_down_weight, down_first_moment, down_second_moment, down_gradient[None, None]
    )
    up_weight_next, up_first_moment_next, up_second_moment_next = adamw_update(
        adapter_up_weight, up_first_moment, up_second_moment, up_gradient[None, None]
    )
    return (
        down_weight_next,
        up_weight_next,
        down_first_moment_next,
        down_second_moment_next,
        up_first_moment_next,
        up_second_moment_next,
    )


def solution(mesh):
    placed = (
        P(None, "dp", "pipe"),
        P(None, "dp", "pipe"),
        P("pipe", None),
        P(None, "dp", None),
        P(),
        P("pipe", "dp", None, None),
        P("pipe", "dp", None, None),
        P("pipe", "dp", None, None),
        P("pipe", "dp", None, None),
        P("pipe", "dp", None, None),
        P("pipe", "dp", None, None),
    )
    return jax.shard_map(
        body,
        mesh=mesh,
        in_specs=placed,
        out_specs=(
            P("pipe", "dp", None, None),
            P("pipe", "dp", None, None),
            P("pipe", "dp", None, None),
            P("pipe", "dp", None, None),
            P("pipe", "dp", None, None),
            P("pipe", "dp", None, None),
        ),
        check_vma=False,
    )
```

profile of v0, /device:TPU:0, one launch (start us, length us, event | category | flops | bytes accessed | tf_op | source)
XLA Modules:
  0.0 784.7 jit_solution(4742045033948489761)
XLA Ops:
  12.0 7.2 reshape.209
  23.4 64.9 %all_to_all.10 = bf16[2,64,4,4096]{3,2,0,1:T(4,128)(2,1)} all-to-all(bf16[2,64,4,4096]{3,2,0,1:T(4,128)(2,1)S(1)} %copy.25), channel_id=1, replica_groups=mesh['pipe'=2,'dp'=64] {'dp'}, dimensions={1} | all-to-all | bytes 8388608 | tf_op jit(solution)/shard_map/all_to_all | solution.py:92
  93.0 7.6 reshape.208
  100.6 4.6 copy.24
  105.2 103.1 %all_to_all.11 = bf16[2,64,4,4096]{3,2,0,1:T(4,128)(2,1)} all-to-all(bf16[2,64,4,4096]{3,2,0,1:T(4,128)(2,1)S(1)} %copy.24), channel_id=1, replica_groups=mesh['pipe'=2,'dp'=64] {'dp'}, dimensions={1} | all-to-all | bytes 8388608 | tf_op jit(solution)/shard_map/all_to_all | solution.py:95
  208.3 27.5 %all-gather.5.cloned.1.call-done = bf16[2,64,4,8192]{3,2,0,1:T(4,128)(2,1)} async-done(((bf16[2,64,4,4096]{3,2,0,1:T(4,128)(2,1)}), bf16[2,64,4,8192]{3,2,0,1:T(4,128)(2,1)}) %all-gather.5.cloned.1.call-update) | async-done | bytes 8388624 | tf_op jit(solution)/shard_map/all_gather | solution.py:100
  235.8 5.0 multiply_reduce_fusion
  240.8 8.3 %multiply_convert_fusion = bf16[1,64,4,8192]{3,2,0,1:T(4,128)(2,1)} fusion(f32[8192]{0:T(1024)S(1)} %bitcast.181, f32[64,4]{1,0:T(8,128)S(1)} %add_rsqrt_fusion, bf16[2,64,4,8192]{3,2,0,1:T(4,128)(2,1)} %all-gather.5.cloned.1.call-done, pred[]{:T(512)S(6)} %eq.62), kind=kLoop, calls=%fused_computation.62 | loop fusion | flops 10485760 | bytes 8422401 | tf_op jit(solution)/shard_map/convert_element_type | solution.py:43
  249.1 7.2 convert_element_type.162
  256.4 10.8 %fusion.144 = (f32[1,64,4,8192]{3,2,0,1:T(4,128)}, bf16[1,64,4,8192]{3,2,0,1:T(4,128)(2,1)}, bf16[1,64,4,8192]{3,2,0,1:T(4,128)(2,1)}) fusion(bf16[2,64,4,8192]{3,2,0,1:T(4,128)(2,1)} %all-gather.5.cloned.1.call-done, pred[]{:T(512)S(6)} %eq.62, pred[]{:T(512)S(6)} %and.20), kind=kLoop, calls=%fused_computation.174 | loop fusion | flops 6291456 | bytes 25165826 | tf_op jit(solution)/shard_map/convert_element_type | solution.py:41
  267.1 10.1 %reshape.210 = f32[256,8192]{1,0:T(8,128)} reshape(f32[1,64,4,8192]{3,2,0,1:T(4,128)} %get-tuple-element.21) | data formatting | bytes 16777216 | tf_op jit(solution)/shard_map/convert_element_type | solution.py:41
  277.2 10.9 %fusion.11 = bf16[256,8192]{1,0:T(8,128)(2,1)} fusion(f32[256,8192]{1,0:T(8,128)} %reshape.210, bf16[256,8192]{1,0:T(8,128)(2,1)} %convert_element_type.162, bf16[1,1,32,8192]{3,2,1,0:T(8,128)(2,1)S(1)} %copy-done.11, bf16[1,1,32,8192]{3,2,1,0:T(8,128)(2,1)S(1)} %copy-done.12), kind=kOutput, calls=%fused_computation.24 | convolution fusion | flops 274735104 | bytes 17825792 | tf_op jit(solution)/shard_map/dot_general | solution.py:128
  292.3 6.9 squeeze.28
  299.2 6.9 select_n.95
  306.1 89.0 %all-gather.3.cloned.1.call-done = bf16[2,64,4,8192]{3,2,0,1:T(4,128)(2,1)} async-done(((bf16[2,64,4,4096]{3,2,0,1:T(4,128)(2,1)}), bf16[2,64,4,8192]{3,2,0,1:T(4,128)(2,1)}) %all-gather.3.cloned.1.call-update) | async-done | bytes 8388624 | tf_op jit(solution)/shard_map/all_gather | solution.py:101
  395.1 8.3 %fusion.147 = (bf16[1,64,4,8192]{3,2,0,1:T(4,128)(2,1)}, bf16[1,64,4,8192]{3,2,0,1:T(4,128)(2,1)}) fusion(bf16[2,64,4,8192]{3,2,0,1:T(4,128)(2,1)} %all-gather.3.cloned.1.call-done, pred[]{:T(512)S(6)} %eq.24), kind=kLoop, calls=%fused_computation.175 | loop fusion | flops 2097152 | bytes 16777216 | tf_op jit(solution)/shard_map/slice | solution.py:142
  403.4 6.9 select_n.90
  413.1 19.5 %collective-permute-done = bf16[256,8192]{1,0:T(8,128)(2,1)} collective-permute-done((bf16[256,8192]{1,0:T(8,128)(2,1)}, bf16[256,8192]{1,0:T(8,128)(2,1)}, u32[]{:S(2)}, u32[]{:S(2)}) %collective-permute-start) | collective-permute-done | bytes 4194336 | tf_op jit(solution)/shard_map/ppermute | solution.py:19
  436.6 10.4 %fusion.12 = bf16[256,8192]{1,0:T(8,128)(2,1)} fusion(bf16[256,8192]{1,0:T(8,128)(2,1)} %get-tuple-element.18, f32[8192]{0:T(1024)S(1)} %bitcast.182, f32[256]{0:T(256)S(1)} %add_rsqrt_fusion.4, bf16[1,1,32,8192]{3,2,1,0:T(8,128)(2,1)S(1)} %copy-done.11, bf16[1,1,32,8192]{3,2,1,0:T(8,128)(2,1)S(1)} %copy-done.12), kind=kOutput, calls=%fused_computation.25 | convolution fusion | flops 285220864 | bytes 9470976 | tf_op jit(solution)/shard_map/dot_general | solution.py:128
  447.0 8.7 %collective-permute-start.1 = (bf16[256,8192]{1,0:T(8,128)(2,1)}, bf16[256,8192]{1,0:T(8,128)(2,1)}, u32[]{:S(2)}, u32[]{:S(2)}) collective-permute-start(bf16[256,8192]{1,0:T(8,128)(2,1)} %fusion.12), channel_id=1, source_target_pairs={{0,64},{1,65},{2,66},{3,67},{4,68},{5,69},{6,70},{7,71},{8,72},{9,... | collective-permute-start | bytes 12582920 | tf_op jit(solution)/shard_map/ppermute | solution.py:19
  459.5 4.9 constant_dynamic-slice_fusion.1
  471.8 71.7 %collective-permute-done.1 = bf16[256,8192]{1,0:T(8,128)(2,1)} collective-permute-done((bf16[256,8192]{1,0:T(8,128)(2,1)}, bf16[256,8192]{1,0:T(8,128)(2,1)}, u32[]{:S(2)}, u32[]{:S(2)}) %collective-permute-start.1) | collective-permute-done | bytes 4194336 | tf_op jit(solution)/shard_map/ppermute | solution.py:19
  543.5 5.9 bitcast_dynamic-update-slice_fusion
  560.8 6.9 squeeze.32
  567.6 85.2 %collective-permute-done.2 = bf16[256,8192]{1,0:T(8,128)(2,1)} collective-permute-done((bf16[256,8192]{1,0:T(8,128)(2,1)}, bf16[256,8192]{1,0:T(8,128)(2,1)}, u32[]{:S(2)}, u32[]{:S(2)}) %collective-permute-start.2) | collective-permute-done | bytes 4194336 | tf_op jit(solution)/shard_map/ppermute | solution.py:19
  662.1 4.7 fusion.31
  672.9 6.5 convolution_multiply_fusion.6
  679.4 4.8 fusion.16
  684.2 6.5 fusion.14
  690.7 68.7 %collective-permute-done.3 = bf16[256,8192]{1,0:T(8,128)(2,1)} collective-permute-done((bf16[256,8192]{1,0:T(8,128)(2,1)}, bf16[256,8192]{1,0:T(8,128)(2,1)}, u32[]{:S(2)}, u32[]{:S(2)}) %collective-permute-start.3) | collective-permute-done | bytes 4194336 | tf_op jit(solution)/shard_map/ppermute | solution.py:19
  759.4 8.6 %fusion.105 = (bf16[1,1,32,8192]{3,2,1,0:T(8,128)(2,1)}, f32[1,1,32,8192]{3,2,1,0:T(8,128)}, f32[1,1,32,8192]{3,2,1,0:T(8,128)}) fusion(bf16[1,1,32,8192]{3,2,1,0:T(8,128)(2,1)S(1)} %copy-done.12, f32[1,1,32,8192]{3,2,1,0:T(8,128)} %param.20, f32[1,1,32,8192]{3,2,1,0:T(8,128)} %param.21, f32[32,8192]{1,0:T(8,128)S(1)} %fusion.14, ...), kind=kOutput, calls=%fused_computation.126 | convolution fusion | flops 283910144 | bytes 19432456 | tf_op jit(solution)/shard_map/sr,sd->rd/dot_general | solution.py:157
  768.1 9.3 %fusion.102 = (bf16[1,1,32,8192]{3,2,1,0:T(8,128)(2,1)}, f32[1,1,32,8192]{3,2,1,0:T(8,128)}, f32[1,1,32,8192]{3,2,1,0:T(8,128)}) fusion(bf16[1,1,32,8192]{3,2,1,0:T(8,128)(2,1)S(1)} %copy-done.11, f32[1,1,32,8192]{3,2,1,0:T(8,128)} %param.18, f32[1,1,32,8192]{3,2,1,0:T(8,128)} %param.19, f32[32,8192]{1,0:T(8,128)} %fusion.16, f32[256]{0:T(256)S(1)} %add_rsqrt_fusion.1, ...), kind=kOutput, calls=%fused_computation.123 | convolution fusion | flops 283918336 | bytes 19432456 | tf_op jit(solution)/shard_map/sr,sd->rd/dot_general | solution.py:160
  (62 shorter events, 62.5 us)
Async XLA Ops:
  7.2 1.6 copy-start
  7.2 228.6 %all-gather.5.cloned.1.call-start = ((), (), s32[]{:S(2)}) async-start(), calls=%async_computation.3 | async-start | bytes 12582912 | tf_op jit(solution)/shard_map/all_gather | solution.py:100
  88.3 1.6 copy-start.13
  88.3 306.8 %all-gather.3.cloned.1.call-start = ((), (), s32[]{:S(2)}) async-start(), calls=%async_computation.2 | async-start | bytes 12582912 | tf_op jit(solution)/shard_map/all_gather | solution.py:101
  208.3 32.5 %copy-start.14 = (f32[1,8192]{1,0:T(1,128)S(1)}, f32[1,8192]{1,0:T(1,128)}, u32[]{:S(2)}) copy-start(f32[1,8192]{1,0:T(1,128)} %param.13) | copy-start | bytes 98308
  267.1 10.1 %copy-start.11 = (bf16[1,1,32,8192]{3,2,1,0:T(8,128)(2,1)S(1)}, bf16[1,1,32,8192]{3,2,1,0:T(8,128)(2,1)}, u32[]{:S(2)}) copy-start(bf16[1,1,32,8192]{3,2,1,0:T(8,128)(2,1)} %param.16) | copy-start | bytes 1572868
  267.1 10.1 %copy-start.12 = (bf16[1,1,32,8192]{3,2,1,0:T(8,128)(2,1)S(1)}, bf16[1,1,32,8192]{3,2,1,0:T(8,128)(2,1)}, u32[]{:S(2)}) copy-start(bf16[1,1,32,8192]{3,2,1,0:T(8,128)(2,1)} %param.17) | copy-start | bytes 1572868
  288.1 144.5 %collective-permute-start = (bf16[256,8192]{1,0:T(8,128)(2,1)}, bf16[256,8192]{1,0:T(8,128)(2,1)}, u32[]{:S(2)}, u32[]{:S(2)}) collective-permute-start(bf16[256,8192]{1,0:T(8,128)(2,1)} %fusion.11), channel_id=1, source_target_pairs={{0,64},{1,65},{2,66},{3,67},{4,68},{5,69},{6,70},{7,71},{8,72},{9,... | collective-permute-start | bytes 12582920 | tf_op jit(solution)/shard_map/ppermute | solution.py:19
  410.3 2.2 copy-start.10
  412.5 20.1 %copy-start.8 = (bf16[256,8192]{1,0:T(8,128)(2,1)S(1)}, bf16[256,8192]{1,0:T(8,128)(2,1)}, u32[]{:S(2)}) copy-start(bf16[256,8192]{1,0:T(8,128)(2,1)} %squeeze.28) | copy-start | bytes 12582916
  413.0 23.5 %copy-start.2 = (bf16[2,256,8192]{2,1,0:T(8,128)(2,1)}, bf16[2,256,8192]{2,1,0:T(8,128)(2,1)S(1)}, u32[]{:S(2)}) copy-start(bf16[2,256,8192]{2,1,0:T(8,128)(2,1)S(1)} %constant_dynamic-update-slice_fusion) | copy-start | bytes 25165828
  447.0 96.5 %collective-permute-start.1 = (bf16[256,8192]{1,0:T(8,128)(2,1)}, bf16[256,8192]{1,0:T(8,128)(2,1)}, u32[]{:S(2)}, u32[]{:S(2)}) collective-permute-start(bf16[256,8192]{1,0:T(8,128)(2,1)} %fusion.12), channel_id=1, source_target_pairs={{0,64},{1,65},{2,66},{3,67},{4,68},{5,69},{6,70},{7,71},{8,72},{9,... | collective-permute-start | bytes 12582920 | tf_op jit(solution)/shard_map/ppermute | solution.py:19
  455.7 8.6 %copy-start.9 = (bf16[256,8192]{1,0:T(8,128)(2,1)S(1)}, bf16[256,8192]{1,0:T(8,128)(2,1)}, u32[]{:S(2)}) copy-start(bf16[256,8192]{1,0:T(8,128)(2,1)} %get-tuple-element.18) | copy-start | bytes 12582916
  459.4 6.2 copy-start.3
  549.4 4.3 copy-start.4
  549.5 5.2 copy-start.7
  559.2 93.6 %collective-permute-start.2 = (bf16[256,8192]{1,0:T(8,128)(2,1)}, bf16[256,8192]{1,0:T(8,128)(2,1)}, u32[]{:S(2)}, u32[]{:S(2)}) collective-permute-start(bf16[256,8192]{1,0:T(8,128)(2,1)} %fusion.22), channel_id=1, source_target_pairs={{64,0},{65,1},{66,2},{67,3},{68,4},{69,5},{70,6},{71,7},{72,8},{73... | collective-permute-start | bytes 12582920 | tf_op jit(solution)/shard_map/ppermute | solution.py:19
  652.8 6.2 copy-start.5
  655.6 6.5 copy-start.6
  666.8 92.7 %collective-permute-start.3 = (bf16[256,8192]{1,0:T(8,128)(2,1)}, bf16[256,8192]{1,0:T(8,128)(2,1)}, u32[]{:S(2)}, u32[]{:S(2)}) collective-permute-start(bf16[256,8192]{1,0:T(8,128)(2,1)} %fusion.31), channel_id=1, source_target_pairs={{64,0},{65,1},{66,2},{67,3},{68,4},{69,5},{70,6},{71,7},{72,8},{73... | collective-permute-start | bytes 12582920 | tf_op jit(solution)/shard_map/ppermute | solution.py:19
  768.1 9.3 %copy-start.1 = (bf16[2,128,4096]{2,1,0:T(8,128)(2,1)S(1)}, bf16[2,128,4096]{2,1,0:T(8,128)(2,1)}, u32[]{:S(2)}) copy-start(bf16[2,128,4096]{2,1,0:T(8,128)(2,1)} %param.11) | copy-start | bytes 6291460
Sparse Core Ops, SparseCore 0:
  88.4 147.3 all-gather.4
  237.5 157.5 all-gather.2
where the time goes:
time: 793 us; the launch traced here: 785 us
  waiting for transfers between devices  362 us (46%)
  blocking collectives  168 us (21%)
  local copies, waits for them, and re-layouts  86.5 us (11%)
  matrix products  78.2 us (10%)
  other arithmetic  59.5 us (8%)
  starting transfers between devices  16.1 us (2%)
  between operations  14.8 us (2%)
    ppermute x4, waiting for transfers between devices, from_behind(): return lax.ppermute(array, axis, pairs)  245 us
    all_to_all x1, blocking collectives, body(): lax.all_to_all(sent_grad.reshape(piece_shape), 'dp', split_axis=1, concat...  103 us
    all_gather x1, waiting for transfers between devices, body(): lax.all_gather(got_grad, 'pipe', axis=3, tiled=True)  89 us
    all_to_all x1, blocking collectives, body(): lax.all_to_all(sent_input.reshape(piece_shape), 'dp', split_axis=1, conca...  64.9 us
    all_gather x1, waiting for transfers between devices, body(): lax.all_gather(got_input, 'pipe', axis=3, tiled=True)  27.5 us
    dot_general x3, matrix products, body(): jnp.einsum('sr,sd->rd', rank_projection, arriving_input, preferred_elemen...  21.6 us
    dot_general x2, matrix products, body(): jnp.dot(rank_projection, up_weight, preferred_element_type=jnp.float32)  21.3 us
    dot_general x3, matrix products, body(): jnp.einsum('sr,sd->rd', rank_projection_gradient, norm_output, preferred_...  18.6 us
  transfers between devices with their start and end apart: 6, of which 6 were waited for; matrix products, arithmetic and copies ran while one was open for 18% of the time, Pallas kernels for 0%

commit v1 on v0

v1 whole, which is shorter than its diff:
```python
import functools

import jax
import jax.numpy as jnp
from jax import lax
from jax.experimental import pallas as pl
from jax.experimental.pallas import tpu as pltpu
from jax.sharding import PartitionSpec as P

adapter_scale = 0.5
beta_one = 0.9
beta_two = 0.999
step_count = 10
learn_rate = 0.001
decay_rate = 0.01
eps_root = 1e-08
eps_norm = 1e-05

MESH = pl.DeviceIdType.MESH
F32 = jnp.float32
BF16 = jnp.bfloat16
RANK = 32
WIDTH = 8192
HALF = 4096
OWNERS = 64
CAP = 4
ROWS = 128
PIECE = 16
GROUPS = 8
MEMBERS = OWNERS // GROUPS
GROUP_ROWS = MEMBERS * PIECE
SPLIT = 4
PART = HALF // SPLIT
AHEAD = 3
STRIDE = 27
TILE = 1024


def partner_of(position):
    dp = lax.axis_index("dp")
    core, x_hi, y, z = dp % 2, (dp // 2) % 2, (dp // 4) % 4, dp // 16
    offset = (STRIDE * position) % OWNERS
    dz, dy, dx, dc = offset // 16, (offset // 4) % 4, (offset // 2) % 2, offset % 2
    dz = (dz + core * (4 - 2 * dz)) % 4
    dy = (dy + core * (4 - 2 * dy)) % 4
    return (((z + dz) % 4 * 4 + (y + dy) % 4) * 2 + (x_hi + dx) % 2) * 2 + (core + dc) % 2


def place_rows(labels_ref, owner_ref):
    lane = lax.broadcasted_iota(jnp.int32, (ROWS, ROWS), 1)
    line = lax.broadcasted_iota(jnp.int32, (ROWS, ROWS), 0)
    owner_row = owner_ref[...].astype(F32)
    parts = []
    for micro in range(2):
        label = jnp.broadcast_to(labels_ref[micro], (ROWS, ROWS)).astype(F32)
        label_row = label.T
        within = jnp.sum(
            jnp.where((label == label_row) & (lane < line), 1.0, 0.0), axis=1, keepdims=True
        )
        target = jnp.sum(
            jnp.where(label[:, :OWNERS] == lane[:, :OWNERS].astype(F32), owner_row, 0.0),
            axis=1,
            keepdims=True,
        )
        slot = jnp.broadcast_to(target * (2 * CAP) + micro * CAP + within, (ROWS, ROWS)).T[:1, :]
        want = lax.broadcasted_iota(jnp.int32, (OWNERS * 2 * CAP, ROWS), 0).astype(F32)
        parts.append(jnp.where(want == slot, 1.0, 0.0))
    return jnp.concatenate(parts, axis=1).astype(BF16)


def row_factors(total_h, total_g, gram):
    dot = functools.partial(jnp.dot, preferred_element_type=F32, precision=lax.Precision.HIGHEST)
    squares = total_h[:, 96:97]
    r0 = lax.rsqrt(squares * (1.0 / WIDTH) + eps_norm)
    low0 = (r0 * total_h[:, 0:32]).astype(BF16).astype(F32)
    moved = dot(low0, gram[32:64, :])
    h1_up0 = total_h[:, 32:64] + adapter_scale * moved[:, 32:64]
    h1_down1 = total_h[:, 64:96] + adapter_scale * moved[:, 64:96]
    squares1 = squares + jnp.sum(
        low0 * (2 * adapter_scale * total_h[:, 32:64] + adapter_scale**2 * moved[:, 32:64]),
        axis=1,
        keepdims=True,
    )
    r1 = lax.rsqrt(jnp.maximum(squares1, 0.0) * (1.0 / WIDTH) + eps_norm)
    low1 = (r1 * h1_down1).astype(BF16).astype(F32)
    lg1 = (adapter_scale * total_g[:, 96:128]).astype(BF16).astype(F32)
    mean = jnp.sum(lg1 * h1_down1, axis=1, keepdims=True) * (1.0 / WIDTH)
    cube = r1 * r1 * r1 * mean
    scaled1 = r1 * lg1
    g1_up0 = total_g[:, 32:64] + dot(scaled1, gram[64:96, :])[:, 32:64] - cube * h1_up0
    lg0 = (adapter_scale * g1_up0).astype(BF16).astype(F32)
    zero = jnp.zeros_like(low0)
    for_h = jnp.concatenate([r0 * lg0, -cube * low0, scaled1, zero], axis=1)
    for_g = jnp.concatenate([zero, low0, zero, low1], axis=1)
    cross_h = jnp.concatenate([zero, low0, zero, zero], axis=1)
    cross_g = jnp.concatenate([zero, zero, scaled1, zero], axis=1)
    return for_h, for_g, cross_h, cross_g


def interleave(upper, lower):
    columns = upper.shape[-1]
    both = jnp.concatenate(
        [upper.reshape(-1, 8, columns), lower.reshape(-1, 8, columns)], axis=1
    )
    return both.astype(BF16)


def gradient_kernel(
    h_hbm,
    g_hbm,
    gain_ref,
    labels_ref,
    owner_ref,
    down_ref,
    up_ref,
    grad_ref,
    h_in,
    g_in,
    send,
    recv,
    weights,
    weights_out,
    products,
    products_in,
    gram,
    total,
    cross,
    grad_out,
    in_sem,
    send_sem,
    recv_sem,
    weight_sem,
    product_send_sem,
    product_sem,
    grad_sem,
):
    pipe = lax.axis_index("pipe")
    dp = lax.axis_index("dp")
    other = (1 - pipe, dp)

    copy_h = pltpu.make_async_copy(h_hbm, h_in, in_sem.at[0])
    copy_g = pltpu.make_async_copy(g_hbm, g_in, in_sem.at[1])
    copy_h.start()
    copy_g.start()

    barrier = pltpu.get_barrier_semaphore()

    @pl.loop(1, OWNERS)
    def _(i):
        pl.semaphore_signal(barrier, inc=1, device_id=(pipe, partner_of(i)), device_id_type=MESH)

    pl.semaphore_signal(barrier, inc=1, device_id=other, device_id_type=MESH)

    mine = pl.ds(pl.multiple_of(pipe * HALF, HALF), HALF)
    theirs = pl.ds(pl.multiple_of((1 - pipe) * HALF, HALF), HALF)
    layer = pl.ds(pl.multiple_of(pipe * 2 * RANK, 2 * RANK), 2 * RANK)
    weights_out[0:RANK, :] = (down_ref[:, theirs].astype(F32) * gain_ref[:, theirs]).astype(BF16)
    weights_out[RANK:, :] = up_ref[:, theirs]
    weights[pl.ds(pl.multiple_of(pipe * 2 * RANK, 2 * RANK), RANK), :] = (
        down_ref[:, mine].astype(F32) * gain_ref[:, mine]
    ).astype(BF16)
    weights[pl.ds(pl.multiple_of(pipe * 2 * RANK + RANK, RANK), RANK), :] = up_ref[:, mine]
    placing = place_rows(labels_ref, owner_ref)
    total[...] = jnp.zeros_like(total)
    cross[...] = jnp.zeros_like(cross)

    copy_h.wait()
    copy_g.wait()
    pl.semaphore_wait(barrier, OWNERS)
    copy_weights = pltpu.make_async_remote_copy(
        src_ref=weights_out,
        dst_ref=weights.at[layer],
        send_sem=weight_sem.at[0],
        recv_sem=weight_sem.at[1],
        device_id=other,
        device_id_type=MESH,
    )
    copy_weights.start()

    def start_part(place, part):
        target = partner_of(place)
        columns = pl.ds(pl.multiple_of(part * PART, PART), PART)
        pltpu.make_async_remote_copy(
            src_ref=send.at[target, :, columns],
            dst_ref=recv.at[place, :, columns],
            send_sem=send_sem,
            recv_sem=recv_sem.at[place // MEMBERS],
            device_id=(pipe, target),
            device_id_type=MESH,
        ).start()

    for part in range(SPLIT):
        columns = slice(part * PART, (part + 1) * PART)
        packed_h = jnp.dot(
            placing, h_in[:, :, columns].reshape(2 * ROWS, PART), preferred_element_type=F32
        )
        packed_g = jnp.dot(
            placing, g_in[:, :, columns].reshape(2 * ROWS, PART), preferred_element_type=F32
        )
        send[:, :, columns] = interleave(packed_h, packed_g)

        @pl.loop(1, AHEAD * MEMBERS)
        def _(i):
            start_part(i, part)

    copy_self = pltpu.make_async_copy(send.at[dp], recv.at[0], recv_sem.at[0])
    copy_self.start()

    def start_products(slot):
        pltpu.make_async_remote_copy(
            src_ref=products.at[slot],
            dst_ref=products_in.at[slot],
            send_sem=product_send_sem,
            recv_sem=product_sem.at[slot],
            device_id=other,
            device_id_type=MESH,
        ).start()

    def wait_products(slot):
        pltpu.make_async_copy(
            products_in.at[slot], products_in.at[slot], product_sem.at[slot]
        ).wait()

    copy_weights.wait()
    products[GROUPS] = lax.dot_general(
        weights[...], weights[...], (((1,), (1,)), ((), ())), preferred_element_type=F32
    )
    start_products(GROUPS)
    wait_products(GROUPS)
    gram[...] = products[GROUPS] + products_in[GROUPS]

    @pl.loop(0, GROUPS + 1)
    def _(group):
        @pl.when(group < GROUPS)
        def _():
            members = pl.ds(group * MEMBERS, MEMBERS)
            pltpu.make_async_copy(recv.at[members], recv.at[members], recv_sem.at[group]).wait()

            @pl.when(group + AHEAD < GROUPS)
            def _():
                @pl.loop(0, SPLIT)
                def _(part):
                    @pl.loop(0, MEMBERS)
                    def _(i):
                        start_part((group + AHEAD) * MEMBERS + i, part)

            product = jnp.zeros((GROUP_ROWS, 4 * RANK), F32)
            squares = jnp.zeros((GROUP_ROWS, ROWS), F32)
            for tile in range(HALF // TILE):
                columns = slice(tile * TILE, (tile + 1) * TILE)
                rows = recv[members, :, columns].reshape(GROUP_ROWS, TILE)
                product += lax.dot_general(
                    rows,
                    weights[:, columns],
                    (((1,), (1,)), ((), ())),
                    preferred_element_type=F32,
                )
                wide = rows.astype(F32)
                for k in range(TILE // ROWS):
                    piece = wide[:, k * ROWS : (k + 1) * ROWS]
                    squares += piece * piece
            line = lax.broadcasted_iota(jnp.int32, product.shape, 0) % PIECE
            lane = lax.broadcasted_iota(jnp.int32, product.shape, 1)
            products[group] = jnp.where(
                (line < 8) & (lane >= 3 * RANK), jnp.sum(squares, axis=1, keepdims=True), product
            )
            start_products(group)

        @pl.when(group > 0)
        def _():
            done = group - 1
            wait_products(done)
            both = (products[done] + products_in[done]).reshape(MEMBERS, PIECE, 4 * RANK)
            for_h, for_g, cross_h, cross_g = row_factors(
                both[:, :8, :].reshape(-1, 4 * RANK), both[:, 8:, :].reshape(-1, 4 * RANK), gram[...]
            )
            factors = interleave(for_h, for_g).reshape(GROUP_ROWS, 4 * RANK)
            beside = interleave(cross_h, cross_g).reshape(GROUP_ROWS, 4 * RANK)
            over_rows = (((0,), (0,)), ((), ()))
            cross[...] += lax.dot_general(factors, beside, over_rows, preferred_element_type=F32)
            members = pl.ds(done * MEMBERS, MEMBERS)
            for tile in range(HALF // TILE):
                columns = slice(tile * TILE, (tile + 1) * TILE)
                rows = recv[members, :, columns].reshape(GROUP_ROWS, TILE)
                total[:, columns] += lax.dot_general(
                    factors, rows, over_rows, preferred_element_type=F32
                )

    line = lax.broadcasted_iota(jnp.int32, cross.shape, 0) // RANK
    lane = lax.broadcasted_iota(jnp.int32, cross.shape, 1) // RANK
    keep = jnp.where((lane == 1) & ((line == 1) | (line == 2)), adapter_scale, 0.0)
    keep = jnp.where((lane == 2) & (line == 1), 1.0, keep)
    cross[...] = cross[...] * keep
    row = lax.broadcasted_iota(jnp.int32, (2 * RANK, TILE), 0)
    scale = jnp.where(row < RANK, 1.0, adapter_scale)

    def finish(tile, section):
        columns = slice(tile * TILE, (tile + 1) * TILE)
        at = pl.ds(pl.multiple_of(section * 2 * RANK, 2 * RANK), 2 * RANK)
        whole = total[at, columns] + jnp.dot(
            cross[at, :].astype(BF16), weights[:, columns], preferred_element_type=F32
        )
        return (whole * scale).astype(BF16)

    sent = []
    for side, section in enumerate((1 - pipe, pipe)):
        for tile in range(HALF // TILE):
            columns = slice(tile * TILE, (tile + 1) * TILE)
            grad_out[side, :, columns] = finish(tile, section)
            placed = grad_ref.at[:, pl.ds(pl.multiple_of(pipe * HALF + tile * TILE, TILE), TILE)]
            if side == 0:
                copy = pltpu.make_async_remote_copy(
                    src_ref=grad_out.at[0, :, columns],
                    dst_ref=placed,
                    send_sem=grad_sem.at[0, tile],
                    recv_sem=grad_sem.at[1, tile],
                    device_id=other,
                    device_id_type=MESH,
                )
            else:
                copy = pltpu.make_async_copy(
                    grad_out.at[1, :, columns], placed, grad_sem.at[2, tile]
                )
            copy.start()
            sent.append(copy)
    pltpu.make_async_copy(send.at[pl.ds(1, 63)], send.at[pl.ds(1, 63)], send_sem).wait()
    pltpu.make_async_copy(products, products, product_send_sem).wait()
    for copy in sent:
        copy.wait()


def gradients(stack_input, output_gradient, gain, labels, owners, down, up):
    anywhere = pl.BlockSpec(memory_space=pl.ANY)
    whole = pl.BlockSpec(memory_space=pltpu.VMEM)
    return pl.pallas_call(
        gradient_kernel,
        out_shape=jax.ShapeDtypeStruct((2 * RANK, WIDTH), BF16),
        in_specs=[anywhere, anywhere, whole, whole, whole, whole, whole],
        out_specs=anywhere,
        scratch_shapes=[
            pltpu.VMEM((2, ROWS, HALF), BF16),
            pltpu.VMEM((2, ROWS, HALF), BF16),
            pltpu.VMEM((OWNERS, PIECE, HALF), BF16),
            pltpu.VMEM((OWNERS, PIECE, HALF), BF16),
            pltpu.VMEM((4 * RANK, HALF), BF16),
            pltpu.VMEM((2 * RANK, HALF), BF16),
            pltpu.VMEM((GROUPS + 1, GROUP_ROWS, 4 * RANK), F32),
            pltpu.VMEM((GROUPS + 1, GROUP_ROWS, 4 * RANK), F32),
            pltpu.VMEM((4 * RANK, 4 * RANK), F32),
            pltpu.VMEM((4 * RANK, HALF), F32),
            pltpu.VMEM((4 * RANK, 4 * RANK), F32),
            pltpu.VMEM((2, 2 * RANK, HALF), BF16),
            pltpu.SemaphoreType.DMA((2,)),
            pltpu.SemaphoreType.DMA(()),
            pltpu.SemaphoreType.DMA((GROUPS,)),
            pltpu.SemaphoreType.DMA((2,)),
            pltpu.SemaphoreType.DMA(()),
            pltpu.SemaphoreType.DMA((GROUPS + 1,)),
            pltpu.SemaphoreType.DMA((3, HALF // TILE)),
        ],
        compiler_params=pltpu.CompilerParams(
            collective_id=0, has_side_effects=True, vmem_limit_bytes=56 * 2**20
        ),
    )(stack_input, output_gradient, gain, labels, owners, down, up)


def adamw_kernel(
    grad_ref,
    gain_ref,
    down_ref,
    up_ref,
    down_m_ref,
    down_v_ref,
    up_m_ref,
    up_v_ref,
    down_out,
    up_out,
    down_m_out,
    down_v_out,
    up_m_out,
    up_v_out,
):
    def update(weight, one, two, gradient, weight_out, one_out, two_out):
        first_new = beta_one * one[...] + (1.0 - beta_one) * gradient
        second_new = beta_two * two[...] + (1.0 - beta_two) * gradient * gradient
        first_hat = first_new / (1.0 - beta_one**step_count)
        second_hat = second_new / (1.0 - beta_two**step_count)
        value = weight[...].astype(F32)
        result = value - learn_rate * (
            first_hat / jnp.sqrt(second_hat + eps_root) + decay_rate * value
        )
        weight_out[...] = result.astype(BF16)
        one_out[...] = first_new
        two_out[...] = second_new

    down_gradient = grad_ref[0:RANK, :].astype(F32) * gain_ref[...]
    update(down_ref, down_m_ref, down_v_ref, down_gradient, down_out, down_m_out, down_v_out)
    update(up_ref, up_m_ref, up_v_ref, grad_ref[RANK:, :].astype(F32), up_out, up_m_out, up_v_out)


def adamw(grad, gain, down, up, down_m, down_v, up_m, up_v):
    tile = 1024
    across = pl.BlockSpec((RANK, tile), lambda j: (0, j))
    shape = lambda dtype: jax.ShapeDtypeStruct((RANK, WIDTH), dtype)
    return pl.pallas_call(
        adamw_kernel,
        grid=(WIDTH // tile,),
        in_specs=[
            pl.BlockSpec((2 * RANK, tile), lambda j: (0, j)),
            pl.BlockSpec((1, tile), lambda j: (0, j)),
        ]
        + [across] * 6,
        out_specs=[across] * 6,
        out_shape=[shape(BF16), shape(BF16), shape(F32), shape(F32), shape(F32), shape(F32)],
    )(grad, gain, down, up, down_m, down_v, up_m, up_v)


def body(
    stack_input,
    output_gradient,
    norm_scale_weight,
    row_adapter_index,
    adapter_owner_index,
    adapter_down_weight,
    adapter_up_weight,
    down_first_moment,
    down_second_moment,
    up_first_moment,
    up_second_moment,
):
    down, up, down_m, down_v, up_m, up_v = (
        array.reshape(RANK, WIDTH)
        for array in (
            adapter_down_weight,
            adapter_up_weight,
            down_first_moment,
            down_second_moment,
            up_first_moment,
            up_second_moment,
        )
    )
    grad = gradients(
        stack_input,
        output_gradient,
        norm_scale_weight,
        row_adapter_index,
        adapter_owner_index.reshape(1, OWNERS),
        down,
        up,
    )
    results = adamw(grad, norm_scale_weight, down, up, down_m, down_v, up_m, up_v)
    return tuple(array.reshape(1, 1, RANK, WIDTH) for array in results)


def solution(mesh):
    by_owner = P("pipe", "dp", None, None)
    return jax.shard_map(
        body,
        mesh=mesh,
        in_specs=(
            P(None, "dp", "pipe"),
            P(None, "dp", "pipe"),
            P("pipe", None),
            P(None, "dp", None),
            P(),
        )
        + (by_owner,) * 6,
        out_specs=(by_owner,) * 6,
        check_vma=False,
    )
```

time: 793 us -> 158 us (0.20)
  waiting for transfers between devices: 362 us -> 0 us
  blocking collectives: 168 us -> 0 us
  Pallas kernels: 0 us -> 155 us
  local copies, waits for them, and re-layouts: 86.5 us -> 1.47 us
  matrix products: 78.2 us -> 0 us
  other arithmetic: 59.5 us -> 0 us
  starting transfers between devices: 16.1 us -> 0 us
  between operations: 14.8 us -> 0.64 us
    ppermute x4 -> x0, waiting for transfers between devices: 245 us -> none  [from_behind(): return lax.ppermute(array, axis, pairs)]
    all_to_all x2 -> x0, blocking collectives: 168 us -> none  [the longest x1 103 us: body(): lax.all_to_all(sent_grad.reshape(piece_shape), 'dp', split_axis=1, concat...]
    pallas_call x0 -> x2, Pallas kernels: none -> 155 us  [the longest x1 147 us: gradients(): pl.pallas_call(gradient_kernel, out_shape=jax.ShapeDtypeStruct((2 * RANK,...]
    all_gather x2 -> x0, waiting for transfers between devices: 116 us -> none  [the longest x1 89 us: body(): lax.all_gather(got_grad, 'pipe', axis=3, tiled=True)]
    dot_general x14 -> x0, matrix products: 78.2 us -> none  [the longest x3 21.6 us: body(): jnp.einsum('sr,sd->rd', rank_projection, arriving_input, preferred_elemen...]
    convert_element_type x5 -> x0, other arithmetic: 28.3 us -> none  [the longest x1 10.8 us: normalize(): value_entries = hidden_state.astype(jnp.float32)]
    reshape x4 -> x0, local copies, waits for them, and re-layouts: 23.5 us -> none  [the longest x2 12.1 us: body(): sent_grad.reshape(piece_shape)]
    convert_element_type x2 -> x0, local copies, waits for them, and re-layouts: 17.3 us -> none  [the longest x1 10.1 us: normalize(): value_entries = hidden_state.astype(jnp.float32)]
  transfers between devices with their start and end apart: 6 -> 0, of which waited for: 6 -> 0; matrix products, arithmetic and copies ran while one was open for 18% -> 0% of each run, Pallas kernels for 0% -> 0%
where the time goes in v1:
time: 158 us; the launch traced here: 157 us
  Pallas kernels  155 us (98%)
    pallas_call x1, Pallas kernels, gradients(): pl.pallas_call(gradient_kernel, out_shape=jax.ShapeDtypeStruct((2 * RANK,...  147 us
    pallas_call x1, Pallas kernels, adamw(): pl.pallas_call(adamw_kernel, grid=(WIDTH // tile,), in_specs=[pl.BlockSpe...  8.05 us

profile of v1, /device:TPU:0, one launch (start us, length us, event | category | flops | bytes accessed | tf_op | source)
XLA Modules:
  0.0 157.3 jit_solution(6116314294371899548)
XLA Ops:
  0.6 1.5 copy.17.labels_ref
  2.1 147.1 %shard_map.154.grad_ref = bf16[64,8192]{1,0:T(8,128)(2,1)} custom-call(bf16[2,128,4096]{2,1,0:T(8,128)(2,1)} %h_hbm.1, bf16[2,128,4096]{2,1,0:T(8,128)(2,1)} %g_hbm.1, f32[1,8192]{1,0:T(1,128)} %gain_ref.3, s32[2,128,1]{2,1,0:T(8,128)} %copy.17.labels_ref, s32[1,64]{1,0:T(1,128)} %bitcast.21, bf16[32,8192]{1,0:T(8,128)(2,1)} %bitcast.13, ...), custom_call_target="tpu_custom_call" | custom-call | tf_op jit(solution)/shard_map/pallas_call | solution.py:335
  149.2 8.0 %shard_map.155 = (bf16[32,8192]{1,0:T(8,128)(2,1)}, bf16[32,8192]{1,0:T(8,128)(2,1)}, f32[32,8192]{1,0:T(8,128)}, f32[32,8192]{1,0:T(8,128)}, f32[32,8192]{1,0:T(8,128)}, /*index=5*/f32[32,8192]{1,0:T(8,128)}) custom-call(bf16[64,8192]{1,0:T(8,128)(2,1)} %shard_map.154.grad_ref, f32[1,8192]{1,0:T(1,128)} %gain_ref.3, bf16[32,8192]{1,0:T(8,128)(2,1)} %bitcast.14, ...), custom_call_target="tpu_custom_call" | custom-call | tf_op jit(solution)/shard_map/pallas_call | solution.py:405

commit v2 on v1

v2 whole, which is shorter than its diff:
```python
import functools

import jax
import jax.numpy as jnp
from jax import lax
from jax.experimental import pallas as pl
from jax.experimental.pallas import tpu as pltpu
from jax.sharding import PartitionSpec as P

adapter_scale = 0.5
beta_one = 0.9
beta_two = 0.999
step_count = 10
learn_rate = 0.001
decay_rate = 0.01
eps_root = 1e-08
eps_norm = 1e-05

MESH = pl.DeviceIdType.MESH
F32 = jnp.float32
BF16 = jnp.bfloat16
RANK = 32
WIDTH = 8192
HALF = 4096
OWNERS = 64
CAP = 4
ROWS = 128
PIECE = 16
GROUPS = 8
MEMBERS = OWNERS // GROUPS
HALF_ROWS = MEMBERS // 2 * PIECE
CROSSED = 8
GROUP_ROWS = MEMBERS * PIECE
SPLIT = 4
PART = HALF // SPLIT
AHEAD = 3
DEFER = 1
TILE = 1024
UPDATE_TILE = 1024


def partner_of(place):
    pipe, dp = lax.axis_index("pipe"), lax.axis_index("dp")
    core, x_hi, y, z = dp % 2, (dp // 2) % 2, (dp // 4) % 4, dp // 16
    group, member = place // MEMBERS, place % MEMBERS
    dx = member // (MEMBERS // 2)
    rank = group * (MEMBERS // 2) + member % (MEMBERS // 2)
    odd = (rank // 16 + dx) % 2
    mixed = (5 * (rank % 16)) % 16
    dz, dc = mixed // 4, mixed % 2
    dy = 2 * ((mixed // 2) % 2) + (odd + dz) % 2
    dz = (dz + core * (4 - 2 * dz)) % 4
    dy = (dy + core * (4 - 2 * dy)) % 4
    target = (((z + dz) % 4 * 4 + (y + dy) % 4) * 2 + (x_hi + dx) % 2) * 2 + (core + dc) % 2
    return (pipe + dx * crossed(group)) % 2, target


def crossed(group):
    return (GROUPS - 1 - group + CROSSED) // GROUPS


def place_rows(labels_ref, owner_ref):
    lane = lax.broadcasted_iota(jnp.int32, (ROWS, ROWS), 1)
    line = lax.broadcasted_iota(jnp.int32, (ROWS, ROWS), 0)
    owner_row = owner_ref[...].astype(F32)
    parts = []
    for micro in range(2):
        label_row = jnp.broadcast_to(labels_ref[micro : micro + 1, :].astype(F32), (ROWS, ROWS))
        label = label_row.T
        within = jnp.sum(
            jnp.where((label == label_row) & (lane < line), 1.0, 0.0), axis=1, keepdims=True
        )
        target = jnp.sum(
            jnp.where(label[:, :OWNERS] == lane[:, :OWNERS].astype(F32), owner_row, 0.0),
            axis=1,
            keepdims=True,
        )
        slot = jnp.broadcast_to(target * (2 * CAP) + micro * CAP + within, (ROWS, ROWS)).T[:1, :]
        want = lax.broadcasted_iota(jnp.int32, (OWNERS * 2 * CAP, ROWS), 0).astype(F32)
        parts.append(jnp.where(want == slot, 1.0, 0.0))
    return jnp.concatenate(parts, axis=1).astype(BF16)


def row_factors(total_h, total_g, gram):
    dot = functools.partial(jnp.dot, preferred_element_type=F32, precision=lax.Precision.HIGHEST)
    squares = total_h[:, 96:97]
    r0 = lax.rsqrt(squares * (1.0 / WIDTH) + eps_norm)
    low0 = (r0 * total_h[:, 0:32]).astype(BF16).astype(F32)
    moved = dot(low0, gram[32:64, :])
    h1_up0 = total_h[:, 32:64] + adapter_scale * moved[:, 32:64]
    h1_down1 = total_h[:, 64:96] + adapter_scale * moved[:, 64:96]
    squares1 = squares + jnp.sum(
        low0 * (2 * adapter_scale * total_h[:, 32:64] + adapter_scale**2 * moved[:, 32:64]),
        axis=1,
        keepdims=True,
    )
    r1 = lax.rsqrt(jnp.maximum(squares1, 0.0) * (1.0 / WIDTH) + eps_norm)
    low1 = (r1 * h1_down1).astype(BF16).astype(F32)
    lg1 = (adapter_scale * total_g[:, 96:128]).astype(BF16).astype(F32)
    mean = jnp.sum(lg1 * h1_down1, axis=1, keepdims=True) * (1.0 / WIDTH)
    cube = r1 * r1 * r1 * mean
    scaled1 = r1 * lg1
    g1_up0 = total_g[:, 32:64] + dot(scaled1, gram[64:96, :])[:, 32:64] - cube * h1_up0
    lg0 = (adapter_scale * g1_up0).astype(BF16).astype(F32)
    zero = jnp.zeros_like(low0)
    for_h = jnp.concatenate([r0 * lg0, -cube * low0, scaled1, zero], axis=1)
    for_g = jnp.concatenate([zero, low0, zero, low1], axis=1)
    cross_h = jnp.concatenate([zero, low0, zero, zero], axis=1)
    cross_g = jnp.concatenate([zero, zero, scaled1, zero], axis=1)
    return for_h, for_g, cross_h, cross_g


def interleave(upper, lower):
    columns = upper.shape[-1]
    both = jnp.concatenate(
        [upper.reshape(-1, 8, columns), lower.reshape(-1, 8, columns)], axis=1
    )
    return both.astype(BF16)


def gradient_kernel(
    h_hbm,
    g_hbm,
    gain_hbm,
    labels_hbm,
    owner_hbm,
    down_hbm,
    up_hbm,
    grad_ref,
    h_in,
    g_in,
    gain_ref,
    labels_ref,
    owner_ref,
    down_ref,
    up_ref,
    send,
    recv,
    weights,
    products,
    products_in,
    gram,
    total,
    cross,
    grad_out,
    grad_in,
    in_sem,
    send_sem,
    recv_sem,
    weight_sem,
    product_send_sem,
    product_sem,
    grad_sem,
):
    pipe = lax.axis_index("pipe")
    dp = lax.axis_index("dp")
    other = (1 - pipe, dp)

    copies_in = [
        pltpu.make_async_copy(*pair, in_sem.at[n])
        for n, pair in enumerate(
            (
                (labels_hbm, labels_ref),
                (owner_hbm, owner_ref),
                (h_hbm, h_in),
                (g_hbm, g_in),
                (gain_hbm, gain_ref),
                (down_hbm, down_ref),
                (up_hbm, up_ref),
            )
        )
    ]
    for copy in copies_in:
        copy.start()

    barrier = pltpu.get_barrier_semaphore()

    @pl.loop(1, OWNERS)
    def _(i):
        pl.semaphore_signal(barrier, inc=1, device_id=partner_of(i), device_id_type=MESH)

    pl.semaphore_signal(barrier, inc=1, device_id=other, device_id_type=MESH)

    layer = pl.ds(pl.multiple_of(pipe * 2 * RANK, 2 * RANK), 2 * RANK)
    copies_in[0].wait()
    copies_in[1].wait()
    placing = place_rows(labels_ref, owner_ref)
    copies_in[2].wait()
    copies_in[3].wait()

    pl.semaphore_wait(barrier, OWNERS)

    def weight_copy(side, part):
        columns = slice(part * PART, (part + 1) * PART)
        return pltpu.make_async_remote_copy(
            src_ref=weights.at[1 - side, layer, columns],
            dst_ref=weights.at[side, layer, columns],
            send_sem=weight_sem.at[0, side, part],
            recv_sem=weight_sem.at[1, side, part],
            device_id=other,
            device_id_type=MESH,
        )

    def start_part(place, part):
        target = partner_of(place)
        columns = pl.ds(pl.multiple_of(part * PART, PART), PART)
        pltpu.make_async_remote_copy(
            src_ref=send.at[target[1], :, columns],
            dst_ref=recv.at[place, :, columns],
            send_sem=send_sem,
            recv_sem=recv_sem.at[place // MEMBERS],
            device_id=target,
            device_id_type=MESH,
        ).start()

    def start_group(group, part, first=0):
        @pl.loop(first, MEMBERS)
        def _(i):
            start_part(group * MEMBERS + i % 2 * (MEMBERS // 2) + i // 2, part)

    def prepare_weights():
        for copy in copies_in[4:]:
            copy.wait()
        for side, half in enumerate((pipe, 1 - pipe)):
            columns = pl.ds(pl.multiple_of(half * HALF, HALF), HALF)
            weights[side, pl.ds(pl.multiple_of(pipe * 2 * RANK, RANK), RANK), :] = (
                down_ref[:, columns].astype(F32) * gain_ref[:, columns]
            ).astype(BF16)
            weights[side, pl.ds(pl.multiple_of(pipe * 2 * RANK + RANK, RANK), RANK), :] = up_ref[
                :, columns
            ]

    for part in range(SPLIT):
        columns = slice(part * PART, (part + 1) * PART)
        packed_h = jnp.dot(
            placing, h_in[:, :, columns].reshape(2 * ROWS, PART), preferred_element_type=F32
        )
        packed_g = jnp.dot(
            placing, g_in[:, :, columns].reshape(2 * ROWS, PART), preferred_element_type=F32
        )
        send[:, :, columns] = interleave(packed_h, packed_g)
        start_group(0, part, 1)
        if part == 0:
            prepare_weights()
        weight_copy(0, part).start()
        weight_copy(1, part).start()

    @pl.loop(1, AHEAD)
    def _(group):
        @pl.loop(0, SPLIT)
        def _(part):
            start_group(group, part)

    copy_self = pltpu.make_async_copy(send.at[dp], recv.at[0], recv_sem.at[0])
    copy_self.start()
    total[...] = jnp.zeros_like(total)
    cross[...] = jnp.zeros_like(cross)

    def start_products(slot):
        pltpu.make_async_remote_copy(
            src_ref=products.at[slot],
            dst_ref=products_in.at[slot],
            send_sem=product_send_sem,
            recv_sem=product_sem.at[slot],
            device_id=other,
            device_id_type=MESH,
        ).start()

    def wait_products(slot):
        pltpu.make_async_copy(
            products_in.at[slot], products_in.at[slot], product_sem.at[slot]
        ).wait()

    for side in range(2):
        for part in range(SPLIT):
            weight_copy(side, part).wait()
    products[GROUPS] = lax.dot_general(
        weights[0], weights[0], (((1,), (1,)), ((), ())), preferred_element_type=F32
    )
    start_products(GROUPS)

    row = lax.broadcasted_iota(jnp.int32, (2 * RANK, TILE), 0)
    scale = jnp.where(row < RANK, 1.0, adapter_scale)

    def mask_cross(side):
        line = lax.broadcasted_iota(jnp.int32, (4 * RANK, 4 * RANK), 0) // RANK
        lane = lax.broadcasted_iota(jnp.int32, (4 * RANK, 4 * RANK), 1) // RANK
        keep = jnp.where((lane == 1) & ((line == 1) | (line == 2)), adapter_scale, 0.0)
        keep = jnp.where((lane == 2) & (line == 1), 1.0, keep)
        cross[side] = cross[side] * keep

    def finish(side, section, columns):
        at = pl.ds(pl.multiple_of(section * 2 * RANK, 2 * RANK), 2 * RANK)
        whole = total[side, at, columns] + jnp.dot(
            cross[side, at, :].astype(BF16),
            weights[side, :, columns],
            preferred_element_type=F32,
        )
        return whole * scale

    def grad_copy(side, tile):
        columns = slice(tile * TILE, (tile + 1) * TILE)
        return pltpu.make_async_remote_copy(
            src_ref=grad_out.at[side, :, columns],
            dst_ref=grad_in.at[side, :, columns],
            send_sem=grad_sem.at[0, side, tile],
            recv_sem=grad_sem.at[1, side, tile],
            device_id=other,
            device_id_type=MESH,
        )

    def hand_over(side):
        mask_cross(side)
        for tile in range(HALF // TILE):
            columns = slice(tile * TILE, (tile + 1) * TILE)
            grad_out[side, :, columns] = finish(side, 1 - pipe, columns).astype(BF16)
            grad_copy(side, tile).start()

    by_rows = (((1,), (1,)), ((), ()))
    over_rows = (((0,), (0,)), ((), ()))

    @pl.loop(0, GROUPS + DEFER)
    def _(group):
        @pl.when(group < GROUPS)
        def _():
            first = group * MEMBERS
            members = pl.ds(first, MEMBERS)
            pltpu.make_async_copy(recv.at[members], recv.at[members], recv_sem.at[group]).wait()
            halves = [
                (pl.ds(first, MEMBERS // 2), 0),
                (pl.ds(first + MEMBERS // 2, MEMBERS // 2), crossed(group)),
            ]
            product = [jnp.zeros((HALF_ROWS, 4 * RANK), F32) for _ in halves]
            squares = [jnp.zeros((HALF_ROWS, ROWS), F32) for _ in halves]
            for tile in range(HALF // TILE):
                columns = slice(tile * TILE, (tile + 1) * TILE)
                for n, (half, side) in enumerate(halves):
                    rows = recv[half, :, columns].reshape(HALF_ROWS, TILE)
                    product[n] += lax.dot_general(
                        rows, weights[side, :, columns], by_rows, preferred_element_type=F32
                    )
                    wide = rows.astype(F32)
                    for k in range(TILE // ROWS):
                        piece = wide[:, k * ROWS : (k + 1) * ROWS]
                        squares[n] += piece * piece
            product = jnp.concatenate(product, axis=0)
            squares = jnp.sum(jnp.concatenate(squares, axis=0), axis=1, keepdims=True)
            line = lax.broadcasted_iota(jnp.int32, product.shape, 0) % PIECE
            lane = lax.broadcasted_iota(jnp.int32, product.shape, 1)
            products[group] = jnp.where((line < 8) & (lane >= 3 * RANK), squares, product)
            start_products(group)

            @pl.when(group + AHEAD < GROUPS)
            def _():
                @pl.loop(0, SPLIT)
                def _(part):
                    start_group(group + AHEAD, part)

        @pl.when(group == DEFER)
        def _():
            wait_products(GROUPS)
            gram[...] = products[GROUPS] + products_in[GROUPS]

        @pl.when(group >= DEFER)
        def _():
            done = group - DEFER
            wait_products(done)
            both = (products[done] + products_in[done]).reshape(MEMBERS, PIECE, 4 * RANK)
            for_h, for_g, cross_h, cross_g = row_factors(
                both[:, :8, :].reshape(-1, 4 * RANK), both[:, 8:, :].reshape(-1, 4 * RANK), gram[...]
            )
            factors = interleave(for_h, for_g).reshape(GROUP_ROWS, 4 * RANK)
            beside = interleave(cross_h, cross_g).reshape(GROUP_ROWS, 4 * RANK)
            first = done * MEMBERS

            def add(rows_at, picked, side):
                cross[side] += lax.dot_general(
                    factors[picked], beside[picked], over_rows, preferred_element_type=F32
                )
                for tile in range(HALF // TILE):
                    columns = slice(tile * TILE, (tile + 1) * TILE)
                    rows = recv[rows_at, :, columns].reshape(-1, TILE)
                    total[side, :, columns] += lax.dot_general(
                        factors[picked], rows, over_rows, preferred_element_type=F32
                    )

            @pl.when(done < CROSSED)
            def _():
                add(pl.ds(first, MEMBERS // 2), slice(0, HALF_ROWS), 0)
                add(pl.ds(first + MEMBERS // 2, MEMBERS // 2), slice(HALF_ROWS, None), 1)

            @pl.when(done >= CROSSED)
            def _():
                add(pl.ds(first, MEMBERS), slice(None), 0)

            @pl.when(done == CROSSED - 1)
            def _():
                hand_over(1)

    hand_over(0)
    for side, half in enumerate((pipe, 1 - pipe)):
        for tile in range(HALF // TILE):
            columns = slice(tile * TILE, (tile + 1) * TILE)
            mine = finish(side, pipe, columns)
            grad_copy(1 - side, tile).wait()
            at = pl.ds(pl.multiple_of(half * HALF + tile * TILE, TILE), TILE)
            grad_ref[:, at] = mine + grad_in[1 - side, :, columns].astype(F32)
    pltpu.make_async_copy(send.at[pl.ds(1, 63)], send.at[pl.ds(1, 63)], send_sem).wait()
    pltpu.make_async_copy(products, products, product_send_sem).wait()


def gradients(stack_input, output_gradient, gain, labels, owners, down, up):
    whole = pl.BlockSpec(memory_space=pltpu.VMEM)
    return pl.pallas_call(
        gradient_kernel,
        out_shape=jax.ShapeDtypeStruct((2 * RANK, WIDTH), F32),
        in_specs=[pl.BlockSpec(memory_space=pl.ANY)] * 7,
        out_specs=whole,
        scratch_shapes=[
            pltpu.VMEM((2, ROWS, HALF), BF16),
            pltpu.VMEM((2, ROWS, HALF), BF16),
            pltpu.VMEM((1, WIDTH), F32),
            pltpu.VMEM((2, ROWS), jnp.int32),
            pltpu.VMEM((1, OWNERS), jnp.int32),
            pltpu.VMEM((RANK, WIDTH), BF16),
            pltpu.VMEM((RANK, WIDTH), BF16),
            pltpu.VMEM((OWNERS, PIECE, HALF), BF16),
            pltpu.VMEM((OWNERS, PIECE, HALF), BF16),
            pltpu.VMEM((2, 4 * RANK, HALF), BF16),
            pltpu.VMEM((GROUPS + 1, GROUP_ROWS, 4 * RANK), F32),
            pltpu.VMEM((GROUPS + 1, GROUP_ROWS, 4 * RANK), F32),
            pltpu.VMEM((4 * RANK, 4 * RANK), F32),
            pltpu.VMEM((2, 4 * RANK, HALF), F32),
            pltpu.VMEM((2, 4 * RANK, 4 * RANK), F32),
            pltpu.VMEM((2, 2 * RANK, HALF), BF16),
            pltpu.VMEM((2, 2 * RANK, HALF), BF16),
            pltpu.SemaphoreType.DMA((7,)),
            pltpu.SemaphoreType.DMA(()),
            pltpu.SemaphoreType.DMA((GROUPS,)),
            pltpu.SemaphoreType.DMA((2, 2, SPLIT)),
            pltpu.SemaphoreType.DMA(()),
            pltpu.SemaphoreType.DMA((GROUPS + 1,)),
            pltpu.SemaphoreType.DMA((2, 2, HALF // TILE)),
        ],
        compiler_params=pltpu.CompilerParams(
            collective_id=0, has_side_effects=True, vmem_limit_bytes=56 * 2**20
        ),
    )(stack_input, output_gradient, gain, labels, owners, down, up)


def adamw_kernel(
    grad_ref,
    gain_ref,
    down_ref,
    up_ref,
    down_m_ref,
    down_v_ref,
    up_m_ref,
    up_v_ref,
    down_out,
    up_out,
    down_m_out,
    down_v_out,
    up_m_out,
    up_v_out,
    weights_new,
    moments_new,
    sem,
):
    outs = ((down_out, down_m_out, down_v_out), (up_out, up_m_out, up_v_out))
    ins = ((down_ref, down_m_ref, down_v_ref), (up_ref, up_m_ref, up_v_ref))

    def copies(tile):
        columns = pl.ds(pl.multiple_of(tile * UPDATE_TILE, UPDATE_TILE), UPDATE_TILE)
        for side in range(2):
            held = (weights_new.at[side], moments_new.at[side, 0], moments_new.at[side, 1])
            for k in range(3):
                yield pltpu.make_async_copy(
                    held[k].at[:, columns], outs[side][k].at[:, columns], sem.at[side, k]
                )

    @pl.loop(0, WIDTH // UPDATE_TILE)
    def _(tile):
        columns = pl.ds(pl.multiple_of(tile * UPDATE_TILE, UPDATE_TILE), UPDATE_TILE)
        for side in range(2):
            gradient = grad_ref[side * RANK : (side + 1) * RANK, columns].astype(F32)
            if side == 0:
                gradient = gradient * gain_ref[:, columns]
            weight, one, two = ins[side]
            first_new = beta_one * one[:, columns] + (1.0 - beta_one) * gradient
            second_new = beta_two * two[:, columns] + (1.0 - beta_two) * gradient * gradient
            value = weight[:, columns].astype(F32)
            step = (first_new * (1.0 / (1.0 - beta_one**step_count))) * lax.rsqrt(
                second_new * (1.0 / (1.0 - beta_two**step_count)) + eps_root
            )
            weights_new[side, :, columns] = (
                value - learn_rate * (step + decay_rate * value)
            ).astype(BF16)
            moments_new[side, 0, :, columns] = first_new
            moments_new[side, 1, :, columns] = second_new
        for copy in copies(tile):
            copy.start()

    for side in range(2):
        held = (weights_new.at[side], moments_new.at[side, 0], moments_new.at[side, 1])
        for k in range(3):
            pltpu.make_async_copy(held[k], held[k], sem.at[side, k]).wait()


def adamw(grad, gain, down, up, down_m, down_v, up_m, up_v):
    shape = lambda dtype: jax.ShapeDtypeStruct((RANK, WIDTH), dtype)
    whole = pl.BlockSpec(memory_space=pltpu.VMEM)
    anywhere = pl.BlockSpec(memory_space=pl.ANY)
    return pl.pallas_call(
        adamw_kernel,
        in_specs=[whole] * 8,
        out_specs=[anywhere] * 6,
        out_shape=[shape(BF16), shape(BF16), shape(F32), shape(F32), shape(F32), shape(F32)],
        scratch_shapes=[
            pltpu.VMEM((2, RANK, WIDTH), BF16),
            pltpu.VMEM((2, 2, RANK, WIDTH), F32),
            pltpu.SemaphoreType.DMA((2, 3)),
        ],
        compiler_params=pltpu.CompilerParams(vmem_limit_bytes=16 * 2**20),
    )(grad, gain, down, up, down_m, down_v, up_m, up_v)


def body(
    stack_input,
    output_gradient,
    norm_scale_weight,
    row_adapter_index,
    adapter_owner_index,
    adapter_down_weight,
    adapter_up_weight,
    down_first_moment,
    down_second_moment,
    up_first_moment,
    up_second_moment,
):
    down, up, down_m, down_v, up_m, up_v = (
        array.reshape(RANK, WIDTH)
        for array in (
            adapter_down_weight,
            adapter_up_weight,
            down_first_moment,
            down_second_moment,
            up_first_moment,
            up_second_moment,
        )
    )
    grad = gradients(
        stack_input,
        output_gradient,
        norm_scale_weight,
        row_adapter_index.reshape(2, ROWS),
        adapter_owner_index.reshape(1, OWNERS),
        down,
        up,
    )
    results = adamw(grad, norm_scale_weight, down, up, down_m, down_v, up_m, up_v)
    return tuple(array.reshape(1, 1, RANK, WIDTH) for array in results)


def solution(mesh):
    by_owner = P("pipe", "dp", None, None)
    return jax.shard_map(
        body,
        mesh=mesh,
        in_specs=(
            P(None, "dp", "pipe"),
            P(None, "dp", "pipe"),
            P("pipe", None),
            P(None, "dp", None),
            P(),
        )
        + (by_owner,) * 6,
        out_specs=(by_owner,) * 6,
        check_vma=False,
    )
```

time: 158 us -> 147 us (0.930)
  Pallas kernels: 155 us -> 143 us
    pallas_call x1, Pallas kernels: 147 us -> 140 us  [gradients(): pl.pallas_call(gradient_kernel, out_shape=jax.ShapeDtypeStruct((2 * RANK,...]
    pallas_call x1, Pallas kernels: 8.05 us -> 2.51 us  [adamw(): pl.pallas_call(adamw_kernel, in_specs=[whole] * 8, out_specs=[anywhere] *...]
where the time goes in v2:
time: 147 us; the launch traced here: 145 us
  Pallas kernels  143 us (97%)
  local copies, waits for them, and re-layouts  1.61 us (1%)
    pallas_call x1, Pallas kernels, gradients(): pl.pallas_call(gradient_kernel, out_shape=jax.ShapeDtypeStruct((2 * RANK,...  140 us

profile of v2, /device:TPU:0, one launch (start us, length us, event | category | flops | bytes accessed | tf_op | source)
XLA Modules:
  0.0 144.9 jit_solution(2142939853384916464)
XLA Ops:
  0.6 0.0 copy-start.1
  0.6 0.0 copy-start.2
  0.7 0.0 copy-start.3
  0.7 0.0 copy-start.4
  0.7 0.0 copy-start.5
  0.7 0.0 copy-start.6
  0.7 0.0 copy-start.7
  0.7 140.0 %shard_map.154.grad_ref = f32[64,8192]{1,0:T(8,128)} custom-call(bf16[2,128,4096]{2,1,0:T(8,128)(2,1)} %h_hbm.1, bf16[2,128,4096]{2,1,0:T(8,128)(2,1)} %g_hbm.1, f32[1,8192]{1,0:T(1,128)} %gain_ref.1, s32[2,128]{1,0:T(2,128)} %bitcast.22, s32[1,64]{1,0:T(1,128)} %bitcast.23, bf16[32,8192]{1,0:T(8,128)(2,1)} %bitcast.14, bf16[32,8192]{1,0:T(8,128)(2,1)} %bitcast.16), custom_call_target="tpu_custom_call" | custom-call | tf_op jit(solution)/shard_map/pallas_call | solution.py:414
  140.7 0.0 copy-done.1
  140.8 0.0 copy-done.2
  140.8 0.0 copy-done.3
  140.8 0.0 copy-done.4
  140.8 0.0 copy-done.5
  140.8 0.0 copy-done.6
  140.8 0.0 copy-done.7
  140.8 0.0 copy-start
  140.8 1.6 %copy-done = f32[64,8192]{1,0:T(8,128)S(1)} copy-done((f32[64,8192]{1,0:T(8,128)S(1)}, f32[64,8192]{1,0:T(8,128)}, u32[]{:S(2)}) %copy-start) | copy-done | bytes 2097176
  142.4 2.5 %shard_map.155 = (bf16[32,8192]{1,0:T(8,128)(2,1)}, bf16[32,8192]{1,0:T(8,128)(2,1)}, f32[32,8192]{1,0:T(8,128)}, f32[32,8192]{1,0:T(8,128)}, f32[32,8192]{1,0:T(8,128)}, /*index=5*/f32[32,8192]{1,0:T(8,128)}) custom-call(f32[64,8192]{1,0:T(8,128)S(1)} %copy-done, f32[1,8192]{1,0:T(1,128)S(1)} %copy-done.7, bf16[32,8192]{1,0:T(8,128)(2,1)S(1)} %bitcast.15, ...), custom_call_target="tpu_custom_call" | custom-call | tf_op jit(solution)/shard_map/pallas_call | solution.py:514
Async XLA Ops:
  0.6 140.1 %copy-start.1 = (bf16[1,1,32,8192]{3,2,1,0:T(8,128)(2,1)S(1)}, bf16[1,1,32,8192]{3,2,1,0:T(8,128)(2,1)}, u32[]{:S(2)}) copy-start(bf16[1,1,32,8192]{3,2,1,0:T(8,128)(2,1)} %param.16) | copy-start | bytes 1572868
  0.6 140.1 %copy-start.2 = (bf16[1,1,32,8192]{3,2,1,0:T(8,128)(2,1)S(1)}, bf16[1,1,32,8192]{3,2,1,0:T(8,128)(2,1)}, u32[]{:S(2)}) copy-start(bf16[1,1,32,8192]{3,2,1,0:T(8,128)(2,1)} %param.17) | copy-start | bytes 1572868
  0.7 140.1 %copy-start.3 = (f32[1,1,32,8192]{3,2,1,0:T(8,128)S(1)}, f32[1,1,32,8192]{3,2,1,0:T(8,128)}, u32[]{:S(2)}) copy-start(f32[1,1,32,8192]{3,2,1,0:T(8,128)} %param.18) | copy-start | bytes 3145732
  0.7 140.1 %copy-start.4 = (f32[1,1,32,8192]{3,2,1,0:T(8,128)S(1)}, f32[1,1,32,8192]{3,2,1,0:T(8,128)}, u32[]{:S(2)}) copy-start(f32[1,1,32,8192]{3,2,1,0:T(8,128)} %param.19) | copy-start | bytes 3145732
  0.7 140.1 %copy-start.5 = (f32[1,1,32,8192]{3,2,1,0:T(8,128)S(1)}, f32[1,1,32,8192]{3,2,1,0:T(8,128)}, u32[]{:S(2)}) copy-start(f32[1,1,32,8192]{3,2,1,0:T(8,128)} %param.20) | copy-start | bytes 3145732
  0.7 140.1 %copy-start.6 = (f32[1,1,32,8192]{3,2,1,0:T(8,128)S(1)}, f32[1,1,32,8192]{3,2,1,0:T(8,128)}, u32[]{:S(2)}) copy-start(f32[1,1,32,8192]{3,2,1,0:T(8,128)} %param.21) | copy-start | bytes 3145732
  0.7 140.1 %copy-start.7 = (f32[1,8192]{1,0:T(1,128)S(1)}, f32[1,8192]{1,0:T(1,128)}, u32[]{:S(2)}) copy-start(f32[1,8192]{1,0:T(1,128)} %gain_ref.1) | copy-start | bytes 98308
  140.8 1.6 %copy-start = (f32[64,8192]{1,0:T(8,128)S(1)}, f32[64,8192]{1,0:T(8,128)}, u32[]{:S(2)}) copy-start(f32[64,8192]{1,0:T(8,128)} %shard_map.154.grad_ref) | copy-start | bytes 6291460

commit v3 on v2

--- a/solution.py
+++ b/solution.py
@@ -29,7 +29,6 @@
 GROUPS = 8
 MEMBERS = OWNERS // GROUPS
 HALF_ROWS = MEMBERS // 2 * PIECE
-CROSSED = 8
 GROUP_ROWS = MEMBERS * PIECE
 SPLIT = 4
 PART = HALF // SPLIT
@@ -39,24 +38,24 @@
 UPDATE_TILE = 1024
 
 
-def partner_of(place):
+def here():
     pipe, dp = lax.axis_index("pipe"), lax.axis_index("dp")
-    core, x_hi, y, z = dp % 2, (dp // 2) % 2, (dp // 4) % 4, dp // 16
-    group, member = place // MEMBERS, place % MEMBERS
-    dx = member // (MEMBERS // 2)
-    rank = group * (MEMBERS // 2) + member % (MEMBERS // 2)
-    odd = (rank // 16 + dx) % 2
-    mixed = (5 * (rank % 16)) % 16
-    dz, dc = mixed // 4, mixed % 2
-    dy = 2 * ((mixed // 2) % 2) + (odd + dz) % 2
-    dz = (dz + core * (4 - 2 * dz)) % 4
-    dy = (dy + core * (4 - 2 * dy)) % 4
-    target = (((z + dz) % 4 * 4 + (y + dy) % 4) * 2 + (x_hi + dx) % 2) * 2 + (core + dc) % 2
-    return (pipe + dx * crossed(group)) % 2, target
-
-
-def crossed(group):
-    return (GROUPS - 1 - group + CROSSED) // GROUPS
+    core, x_hi = lax.rem(dp, 2), lax.rem(lax.div(dp, 2), 2)
+    return pipe, core, x_hi, lax.rem(lax.div(dp, 4), 4) + 4, lax.div(dp, 16) + 4, 1 - 2 * core
+
+
+def partner_of(place, at):
+    pipe, core, x_hi, y, z, sense = at
+    member = lax.rem(place, MEMBERS)
+    dx = lax.div(member, MEMBERS // 2)
+    rank = lax.div(place, MEMBERS) * (MEMBERS // 2) + lax.rem(member, MEMBERS // 2)
+    mixed = lax.rem(5 * rank, 16)
+    dz = lax.div(mixed, 4)
+    dy = 2 * lax.rem(lax.div(mixed, 2), 2) + lax.rem(lax.div(rank, 16) + dx + dz, 2)
+    z = lax.rem(z + sense * dz, 4)
+    y = lax.rem(y + sense * dy, 4)
+    target = z * 16 + y * 4 + lax.rem(x_hi + dx, 2) * 2 + lax.rem(core + mixed, 2)
+    return lax.rem(pipe + dx, 2), target
 
 
 def place_rows(labels_ref, owner_ref):
@@ -175,9 +174,15 @@
 
     barrier = pltpu.get_barrier_semaphore()
 
+    at = here()
+
     @pl.loop(1, OWNERS)
     def _(i):
-        pl.semaphore_signal(barrier, inc=1, device_id=partner_of(i), device_id_type=MESH)
+        target = lax.rem(dp + i, OWNERS)
+        same = 1 - lax.rem(lax.div(target, 2) + at[2], 2)
+        pl.semaphore_signal(
+            barrier, inc=1, device_id=(lax.rem(pipe + 1 - same, 2), target), device_id_type=MESH
+        )
 
     pl.semaphore_signal(barrier, inc=1, device_id=other, device_id_type=MESH)
 
@@ -202,13 +207,13 @@
         )
 
     def start_part(place, part):
-        target = partner_of(place)
+        target = partner_of(place, at)
         columns = pl.ds(pl.multiple_of(part * PART, PART), PART)
         pltpu.make_async_remote_copy(
             src_ref=send.at[target[1], :, columns],
             dst_ref=recv.at[place, :, columns],
             send_sem=send_sem,
-            recv_sem=recv_sem.at[place // MEMBERS],
+            recv_sem=recv_sem.at[lax.div(place, MEMBERS)],
             device_id=target,
             device_id_type=MESH,
         ).start()
@@ -216,7 +221,9 @@
     def start_group(group, part, first=0):
         @pl.loop(first, MEMBERS)
         def _(i):
-            start_part(group * MEMBERS + i % 2 * (MEMBERS // 2) + i // 2, part)
+            start_part(
+                group * MEMBERS + lax.rem(i, 2) * (MEMBERS // 2) + lax.div(i, 2), part
+            )
 
     def prepare_weights():
         for copy in copies_in[4:]:
@@ -328,7 +335,7 @@
             pltpu.make_async_copy(recv.at[members], recv.at[members], recv_sem.at[group]).wait()
             halves = [
                 (pl.ds(first, MEMBERS // 2), 0),
-                (pl.ds(first + MEMBERS // 2, MEMBERS // 2), crossed(group)),
+                (pl.ds(first + MEMBERS // 2, MEMBERS // 2), 1),
             ]
             product = [jnp.zeros((HALF_ROWS, 4 * RANK), F32) for _ in halves]
             squares = [jnp.zeros((HALF_ROWS, ROWS), F32) for _ in halves]
@@ -384,19 +391,10 @@
                         factors[picked], rows, over_rows, preferred_element_type=F32
                     )
 
-            @pl.when(done < CROSSED)
-            def _():
-                add(pl.ds(first, MEMBERS // 2), slice(0, HALF_ROWS), 0)
-                add(pl.ds(first + MEMBERS // 2, MEMBERS // 2), slice(HALF_ROWS, None), 1)
-
-            @pl.when(done >= CROSSED)
-            def _():
-                add(pl.ds(first, MEMBERS), slice(None), 0)
-
-            @pl.when(done == CROSSED - 1)
-            def _():
-                hand_over(1)
-
+            add(pl.ds(first, MEMBERS // 2), slice(0, HALF_ROWS), 0)
+            add(pl.ds(first + MEMBERS // 2, MEMBERS // 2), slice(HALF_ROWS, None), 1)
+
+    hand_over(1)
     hand_over(0)
     for side, half in enumerate((pipe, 1 - pipe)):
         for tile in range(HALF // TILE):

time: 147 us -> 142 us (0.966); the launches traced: 145 us -> 142 us
  Pallas kernels: 143 us -> 139 us
    pallas_call x1, Pallas kernels: 140 us -> 137 us  [gradients(): pl.pallas_call(gradient_kernel, out_shape=jax.ShapeDtypeStruct((2 * RANK,...]
where the time goes in v3:
time: 142 us
  Pallas kernels  139 us (98%)
  local copies, waits for them, and re-layouts  1.61 us (1%)
    pallas_call x1, Pallas kernels, gradients(): pl.pallas_call(gradient_kernel, out_shape=jax.ShapeDtypeStruct((2 * RANK,...  137 us

profile of v3, /device:TPU:0, one launch (start us, length us, event | category | flops | bytes accessed | tf_op | source)
XLA Modules:
  0.0 141.9 jit_solution(2004468602314262072)
XLA Ops:
  0.6 0.0 copy-start.1
  0.6 0.0 copy-start.2
  0.7 0.0 copy-start.3
  0.7 0.0 copy-start.4
  0.7 0.0 copy-start.5
  0.7 0.0 copy-start.6
  0.7 0.0 copy-start.7
  0.7 137.0 %shard_map.154.grad_ref = f32[64,8192]{1,0:T(8,128)} custom-call(bf16[2,128,4096]{2,1,0:T(8,128)(2,1)} %h_hbm.1, bf16[2,128,4096]{2,1,0:T(8,128)(2,1)} %g_hbm.1, f32[1,8192]{1,0:T(1,128)} %gain_ref.1, s32[2,128]{1,0:T(2,128)} %bitcast.22, s32[1,64]{1,0:T(1,128)} %bitcast.23, bf16[32,8192]{1,0:T(8,128)(2,1)} %bitcast.14, bf16[32,8192]{1,0:T(8,128)(2,1)} %bitcast.16), custom_call_target="tpu_custom_call" | custom-call | tf_op jit(solution)/shard_map/pallas_call | solution.py:412
  137.7 0.0 copy-done.1
  137.7 0.0 copy-done.2
  137.7 0.0 copy-done.3
  137.7 0.0 copy-done.4
  137.7 0.0 copy-done.5
  137.8 0.0 copy-done.6
  137.8 0.0 copy-done.7
  137.8 0.0 copy-start
  137.8 1.6 %copy-done = f32[64,8192]{1,0:T(8,128)S(1)} copy-done((f32[64,8192]{1,0:T(8,128)S(1)}, f32[64,8192]{1,0:T(8,128)}, u32[]{:S(2)}) %copy-start) | copy-done | bytes 2097176
  139.4 2.5 %shard_map.155 = (bf16[32,8192]{1,0:T(8,128)(2,1)}, bf16[32,8192]{1,0:T(8,128)(2,1)}, f32[32,8192]{1,0:T(8,128)}, f32[32,8192]{1,0:T(8,128)}, f32[32,8192]{1,0:T(8,128)}, /*index=5*/f32[32,8192]{1,0:T(8,128)}) custom-call(f32[64,8192]{1,0:T(8,128)S(1)} %copy-done, f32[1,8192]{1,0:T(1,128)S(1)} %copy-done.7, bf16[32,8192]{1,0:T(8,128)(2,1)S(1)} %bitcast.15, ...), custom_call_target="tpu_custom_call" | custom-call | tf_op jit(solution)/shard_map/pallas_call | solution.py:512
Async XLA Ops:
  0.6 137.1 %copy-start.1 = (bf16[1,1,32,8192]{3,2,1,0:T(8,128)(2,1)S(1)}, bf16[1,1,32,8192]{3,2,1,0:T(8,128)(2,1)}, u32[]{:S(2)}) copy-start(bf16[1,1,32,8192]{3,2,1,0:T(8,128)(2,1)} %param.16) | copy-start | bytes 1572868
  0.6 137.1 %copy-start.2 = (bf16[1,1,32,8192]{3,2,1,0:T(8,128)(2,1)S(1)}, bf16[1,1,32,8192]{3,2,1,0:T(8,128)(2,1)}, u32[]{:S(2)}) copy-start(bf16[1,1,32,8192]{3,2,1,0:T(8,128)(2,1)} %param.17) | copy-start | bytes 1572868
  0.7 137.1 %copy-start.3 = (f32[1,1,32,8192]{3,2,1,0:T(8,128)S(1)}, f32[1,1,32,8192]{3,2,1,0:T(8,128)}, u32[]{:S(2)}) copy-start(f32[1,1,32,8192]{3,2,1,0:T(8,128)} %param.18) | copy-start | bytes 3145732
  0.7 137.1 %copy-start.4 = (f32[1,1,32,8192]{3,2,1,0:T(8,128)S(1)}, f32[1,1,32,8192]{3,2,1,0:T(8,128)}, u32[]{:S(2)}) copy-start(f32[1,1,32,8192]{3,2,1,0:T(8,128)} %param.19) | copy-start | bytes 3145732
  0.7 137.1 %copy-start.5 = (f32[1,1,32,8192]{3,2,1,0:T(8,128)S(1)}, f32[1,1,32,8192]{3,2,1,0:T(8,128)}, u32[]{:S(2)}) copy-start(f32[1,1,32,8192]{3,2,1,0:T(8,128)} %param.20) | copy-start | bytes 3145732
  0.7 137.1 %copy-start.6 = (f32[1,1,32,8192]{3,2,1,0:T(8,128)S(1)}, f32[1,1,32,8192]{3,2,1,0:T(8,128)}, u32[]{:S(2)}) copy-start(f32[1,1,32,8192]{3,2,1,0:T(8,128)} %param.21) | copy-start | bytes 3145732
  0.7 137.1 %copy-start.7 = (f32[1,8192]{1,0:T(1,128)S(1)}, f32[1,8192]{1,0:T(1,128)}, u32[]{:S(2)}) copy-start(f32[1,8192]{1,0:T(1,128)} %gain_ref.1) | copy-start | bytes 98308
  137.8 1.6 %copy-start = (f32[64,8192]{1,0:T(8,128)S(1)}, f32[64,8192]{1,0:T(8,128)}, u32[]{:S(2)}) copy-start(f32[64,8192]{1,0:T(8,128)} %shard_map.154.grad_ref) | copy-start | bytes 6291460

commit v4 on v3

--- a/solution.py
+++ b/solution.py
@@ -33,7 +33,6 @@
 SPLIT = 4
 PART = HALF // SPLIT
 AHEAD = 3
-DEFER = 1
 TILE = 1024
 UPDATE_TILE = 1024
 
@@ -125,7 +124,7 @@
     owner_hbm,
     down_hbm,
     up_hbm,
-    grad_ref,
+    grad_hbm,
     h_in,
     g_in,
     gain_ref,
@@ -143,6 +142,7 @@
     cross,
     grad_out,
     grad_in,
+    grad_whole,
     in_sem,
     send_sem,
     recv_sem,
@@ -150,6 +150,7 @@
     product_send_sem,
     product_sem,
     grad_sem,
+    out_sem,
 ):
     pipe = lax.axis_index("pipe")
     dp = lax.axis_index("dp")
@@ -326,94 +327,104 @@
     by_rows = (((1,), (1,)), ((), ()))
     over_rows = (((0,), (0,)), ((), ()))
 
-    @pl.loop(0, GROUPS + DEFER)
-    def _(group):
-        @pl.when(group < GROUPS)
-        def _():
-            first = group * MEMBERS
-            members = pl.ds(first, MEMBERS)
-            pltpu.make_async_copy(recv.at[members], recv.at[members], recv_sem.at[group]).wait()
-            halves = [
-                (pl.ds(first, MEMBERS // 2), 0),
-                (pl.ds(first + MEMBERS // 2, MEMBERS // 2), 1),
-            ]
-            product = [jnp.zeros((HALF_ROWS, 4 * RANK), F32) for _ in halves]
-            squares = [jnp.zeros((HALF_ROWS, ROWS), F32) for _ in halves]
+    def use_factors(done, finished):
+        wait_products(done)
+        both = (products[done] + products_in[done]).reshape(MEMBERS, PIECE, 4 * RANK)
+        for_h, for_g, cross_h, cross_g = row_factors(
+            both[:, :8, :].reshape(-1, 4 * RANK), both[:, 8:, :].reshape(-1, 4 * RANK), gram[...]
+        )
+        factors = interleave(for_h, for_g).reshape(GROUP_ROWS, 4 * RANK)
+        beside = interleave(cross_h, cross_g).reshape(GROUP_ROWS, 4 * RANK)
+        first = done * MEMBERS
+
+        def add(rows_at, picked, side):
+            cross[side] += lax.dot_general(
+                factors[picked], beside[picked], over_rows, preferred_element_type=F32
+            )
             for tile in range(HALF // TILE):
                 columns = slice(tile * TILE, (tile + 1) * TILE)
-                for n, (half, side) in enumerate(halves):
-                    rows = recv[half, :, columns].reshape(HALF_ROWS, TILE)
-                    product[n] += lax.dot_general(
-                        rows, weights[side, :, columns], by_rows, preferred_element_type=F32
-                    )
-                    wide = rows.astype(F32)
-                    for k in range(TILE // ROWS):
-                        piece = wide[:, k * ROWS : (k + 1) * ROWS]
-                        squares[n] += piece * piece
-            product = jnp.concatenate(product, axis=0)
-            squares = jnp.sum(jnp.concatenate(squares, axis=0), axis=1, keepdims=True)
-            line = lax.broadcasted_iota(jnp.int32, product.shape, 0) % PIECE
-            lane = lax.broadcasted_iota(jnp.int32, product.shape, 1)
-            products[group] = jnp.where((line < 8) & (lane >= 3 * RANK), squares, product)
-            start_products(group)
-
-            @pl.when(group + AHEAD < GROUPS)
-            def _():
-                @pl.loop(0, SPLIT)
-                def _(part):
-                    start_group(group + AHEAD, part)
-
-        @pl.when(group == DEFER)
+                rows = recv[rows_at, :, columns].reshape(-1, TILE)
+                total[side, :, columns] += lax.dot_general(
+                    factors[picked], rows, over_rows, preferred_element_type=F32
+                )
+
+        add(pl.ds(first + MEMBERS // 2, MEMBERS // 2), slice(HALF_ROWS, None), 1)
+        if finished:
+            hand_over(1)
+        add(pl.ds(first, MEMBERS // 2), slice(0, HALF_ROWS), 0)
+        if finished:
+            hand_over(0)
+
+    @pl.loop(0, GROUPS)
+    def _(group):
+        first = group * MEMBERS
+        members = pl.ds(first, MEMBERS)
+        pltpu.make_async_copy(recv.at[members], recv.at[members], recv_sem.at[group]).wait()
+        halves = [
+            (pl.ds(first, MEMBERS // 2), 0),
+            (pl.ds(first + MEMBERS // 2, MEMBERS // 2), 1),
+        ]
+        product = [jnp.zeros((HALF_ROWS, 4 * RANK), F32) for _ in halves]
+        squares = [jnp.zeros((HALF_ROWS, ROWS), F32) for _ in halves]
+        for tile in range(HALF // TILE):
+            columns = slice(tile * TILE, (tile + 1) * TILE)
+            for n, (half, side) in enumerate(halves):
+                rows = recv[half, :, columns].reshape(HALF_ROWS, TILE)
+                product[n] += lax.dot_general(
+                    rows, weights[side, :, columns], by_rows, preferred_element_type=F32
+                )
+                wide = rows.astype(F32)
+                for k in range(TILE // ROWS):
+                    piece = wide[:, k * ROWS : (k + 1) * ROWS]
+                    squares[n] += piece * piece
+        product = jnp.concatenate(product, axis=0)
+        squares = jnp.sum(jnp.concatenate(squares, axis=0), axis=1, keepdims=True)
+        line = lax.broadcasted_iota(jnp.int32, product.shape, 0) % PIECE
+        lane = lax.broadcasted_iota(jnp.int32, product.shape, 1)
+        products[group] = jnp.where((line < 8) & (lane >= 3 * RANK), squares, product)
+        start_products(group)
+
+        @pl.when(group + AHEAD < GROUPS)
+        def _():
+            @pl.loop(0, SPLIT)
+            def _(part):
+                start_group(group + AHEAD, part)
+
+        @pl.when(group == 1)
         def _():
             wait_products(GROUPS)
             gram[...] = products[GROUPS] + products_in[GROUPS]
 
-        @pl.when(group >= DEFER)
+        @pl.when(group >= 1)
         def _():
-            done = group - DEFER
-            wait_products(done)
-            both = (products[done] + products_in[done]).reshape(MEMBERS, PIECE, 4 * RANK)
-            for_h, for_g, cross_h, cross_g = row_factors(
-                both[:, :8, :].reshape(-1, 4 * RANK), both[:, 8:, :].reshape(-1, 4 * RANK), gram[...]
-            )
-            factors = interleave(for_h, for_g).reshape(GROUP_ROWS, 4 * RANK)
-            beside = interleave(cross_h, cross_g).reshape(GROUP_ROWS, 4 * RANK)
-            first = done * MEMBERS
-
-            def add(rows_at, picked, side):
-                cross[side] += lax.dot_general(
-                    factors[picked], beside[picked], over_rows, preferred_element_type=F32
-                )
-                for tile in range(HALF // TILE):
-                    columns = slice(tile * TILE, (tile + 1) * TILE)
-                    rows = recv[rows_at, :, columns].reshape(-1, TILE)
-                    total[side, :, columns] += lax.dot_general(
-                        factors[picked], rows, over_rows, preferred_element_type=F32
-                    )
-
-            add(pl.ds(first, MEMBERS // 2), slice(0, HALF_ROWS), 0)
-            add(pl.ds(first + MEMBERS // 2, MEMBERS // 2), slice(HALF_ROWS, None), 1)
-
-    hand_over(1)
-    hand_over(0)
+            use_factors(group - 1, False)
+
+    use_factors(GROUPS - 1, True)
+    copies_out = []
     for side, half in enumerate((pipe, 1 - pipe)):
         for tile in range(HALF // TILE):
             columns = slice(tile * TILE, (tile + 1) * TILE)
             mine = finish(side, pipe, columns)
             grad_copy(1 - side, tile).wait()
             at = pl.ds(pl.multiple_of(half * HALF + tile * TILE, TILE), TILE)
-            grad_ref[:, at] = mine + grad_in[1 - side, :, columns].astype(F32)
+            grad_whole[side, :, columns] = mine + grad_in[1 - side, :, columns].astype(F32)
+            copy = pltpu.make_async_copy(
+                grad_whole.at[side, :, columns], grad_hbm.at[:, at], out_sem.at[side, tile]
+            )
+            copy.start()
+            copies_out.append(copy)
     pltpu.make_async_copy(send.at[pl.ds(1, 63)], send.at[pl.ds(1, 63)], send_sem).wait()
     pltpu.make_async_copy(products, products, product_send_sem).wait()
+    for copy in copies_out:
+        copy.wait()
 
 
 def gradients(stack_input, output_gradient, gain, labels, owners, down, up):
-    whole = pl.BlockSpec(memory_space=pltpu.VMEM)
     return pl.pallas_call(
         gradient_kernel,
         out_shape=jax.ShapeDtypeStruct((2 * RANK, WIDTH), F32),
         in_specs=[pl.BlockSpec(memory_space=pl.ANY)] * 7,
-        out_specs=whole,
+        out_specs=pl.BlockSpec(memory_space=pl.ANY),
         scratch_shapes=[
             pltpu.VMEM((2, ROWS, HALF), BF16),
             pltpu.VMEM((2, ROWS, HALF), BF16),
@@ -432,6 +443,7 @@
             pltpu.VMEM((2, 4 * RANK, 4 * RANK), F32),
             pltpu.VMEM((2, 2 * RANK, HALF), BF16),
             pltpu.VMEM((2, 2 * RANK, HALF), BF16),
+            pltpu.VMEM((2, 2 * RANK, HALF), F32),
             pltpu.SemaphoreType.DMA((7,)),
             pltpu.SemaphoreType.DMA(()),
             pltpu.SemaphoreType.DMA((GROUPS,)),
@@ -439,6 +451,7 @@
             pltpu.SemaphoreType.DMA(()),
             pltpu.SemaphoreType.DMA((GROUPS + 1,)),
             pltpu.SemaphoreType.DMA((2, 2, HALF // TILE)),
+            pltpu.SemaphoreType.DMA((2, HALF // TILE)),
         ],
         compiler_params=pltpu.CompilerParams(
             collective_id=0, has_side_effects=True, vmem_limit_bytes=56 * 2**20
@@ -447,7 +460,7 @@
 
 
 def adamw_kernel(
-    grad_ref,
+    grad_hbm,
     gain_ref,
     down_ref,
     up_ref,
@@ -463,7 +476,9 @@
     up_v_out,
     weights_new,
     moments_new,
+    grad_ref,
     sem,
+    in_sem,
 ):
     outs = ((down_out, down_m_out, down_v_out), (up_out, up_m_out, up_v_out))
     ins = ((down_ref, down_m_ref, down_v_ref), (up_ref, up_m_ref, up_v_ref))
@@ -477,9 +492,20 @@
                     held[k].at[:, columns], outs[side][k].at[:, columns], sem.at[side, k]
                 )
 
+    def grad_in(tile):
+        columns = pl.ds(pl.multiple_of(tile * UPDATE_TILE, UPDATE_TILE), UPDATE_TILE)
+        return pltpu.make_async_copy(
+            grad_hbm.at[:, columns], grad_ref.at[:, columns], in_sem.at[tile]
+        )
+
+    @pl.loop(0, WIDTH // UPDATE_TILE)
+    def _(tile):
+        grad_in(tile).start()
+
     @pl.loop(0, WIDTH // UPDATE_TILE)
     def _(tile):
         columns = pl.ds(pl.multiple_of(tile * UPDATE_TILE, UPDATE_TILE), UPDATE_TILE)
+        grad_in(tile).wait()
         for side in range(2):
             gradient = grad_ref[side * RANK : (side + 1) * RANK, columns].astype(F32)
             if side == 0:
@@ -511,15 +537,17 @@
     anywhere = pl.BlockSpec(memory_space=pl.ANY)
     return pl.pallas_call(
         adamw_kernel,
-        in_specs=[whole] * 8,
+        in_specs=[anywhere] + [whole] * 7,
         out_specs=[anywhere] * 6,
         out_shape=[shape(BF16), shape(BF16), shape(F32), shape(F32), shape(F32), shape(F32)],
         scratch_shapes=[
             pltpu.VMEM((2, RANK, WIDTH), BF16),
             pltpu.VMEM((2, 2, RANK, WIDTH), F32),
+            pltpu.VMEM((2 * RANK, WIDTH), F32),
             pltpu.SemaphoreType.DMA((2, 3)),
+            pltpu.SemaphoreType.DMA((WIDTH // UPDATE_TILE,)),
         ],
-        compiler_params=pltpu.CompilerParams(vmem_limit_bytes=16 * 2**20),
+        compiler_params=pltpu.CompilerParams(vmem_limit_bytes=48 * 2**20),
     )(grad, gain, down, up, down_m, down_v, up_m, up_v)
 
 

time: 142 us -> 140 us (0.986)
  local copies, waits for them, and re-layouts: 1.61 us -> 0.03 us
    unnamed x16 -> x14, local copies, waits for them, and re-layouts: 1.61 us -> 0.03 us
where the time goes in v4:
time: 140 us
  Pallas kernels  140 us (100%)
    pallas_call x1, Pallas kernels, gradients(): pl.pallas_call(gradient_kernel, out_shape=jax.ShapeDtypeStruct((2 * RANK,...  136 us
    pallas_call x1, Pallas kernels, adamw(): pl.pallas_call(adamw_kernel, in_specs=[anywhere] + [whole] * 7, out_specs...  3.55 us

profile of v4, /device:TPU:0, one launch (start us, length us, event | category | flops | bytes accessed | tf_op | source)
XLA Modules:
  0.0 140.3 jit_solution(17849939295809098376)
XLA Ops:
  0.6 0.0 copy-start
  0.6 0.0 copy-start.1
  0.7 0.0 copy-start.2
  0.7 0.0 copy-start.3
  0.7 0.0 copy-start.4
  0.7 0.0 copy-start.5
  0.7 0.0 copy-start.6
  0.7 135.9 %shard_map.154.grad_hbm = f32[64,8192]{1,0:T(8,128)} custom-call(bf16[2,128,4096]{2,1,0:T(8,128)(2,1)} %h_hbm.1, bf16[2,128,4096]{2,1,0:T(8,128)(2,1)} %g_hbm.1, f32[1,8192]{1,0:T(1,128)} %gain_ref.1, s32[2,128]{1,0:T(2,128)} %bitcast.22, s32[1,64]{1,0:T(1,128)} %bitcast.23, bf16[32,8192]{1,0:T(8,128)(2,1)} %bitcast.14, bf16[32,8192]{1,0:T(8,128)(2,1)} %bitcast.16), custom_call_target="tpu_custom_call" | custom-call | tf_op jit(solution)/shard_map/pallas_call | solution.py:423
  136.7 0.0 copy-done
  136.7 0.0 copy-done.1
  136.7 0.0 copy-done.2
  136.7 0.0 copy-done.3
  136.7 0.0 copy-done.4
  136.7 0.0 copy-done.5
  136.7 0.0 copy-done.6
  136.7 3.6 %shard_map.155 = (bf16[32,8192]{1,0:T(8,128)(2,1)}, bf16[32,8192]{1,0:T(8,128)(2,1)}, f32[32,8192]{1,0:T(8,128)}, f32[32,8192]{1,0:T(8,128)}, f32[32,8192]{1,0:T(8,128)}, /*index=5*/f32[32,8192]{1,0:T(8,128)}) custom-call(f32[64,8192]{1,0:T(8,128)} %shard_map.154.grad_hbm, f32[1,8192]{1,0:T(1,128)S(1)} %copy-done.6, bf16[32,8192]{1,0:T(8,128)(2,1)S(1)} %bitcast.15, ...), custom_call_target="tpu_custom_call" | custom-call | tf_op jit(solution)/shard_map/pallas_call | solution.py:538
Async XLA Ops:
  0.6 136.0 %copy-start = (bf16[1,1,32,8192]{3,2,1,0:T(8,128)(2,1)S(1)}, bf16[1,1,32,8192]{3,2,1,0:T(8,128)(2,1)}, u32[]{:S(2)}) copy-start(bf16[1,1,32,8192]{3,2,1,0:T(8,128)(2,1)} %param.16) | copy-start | bytes 1572868
  0.6 136.0 %copy-start.1 = (bf16[1,1,32,8192]{3,2,1,0:T(8,128)(2,1)S(1)}, bf16[1,1,32,8192]{3,2,1,0:T(8,128)(2,1)}, u32[]{:S(2)}) copy-start(bf16[1,1,32,8192]{3,2,1,0:T(8,128)(2,1)} %param.17) | copy-start | bytes 1572868
  0.7 136.0 %copy-start.2 = (f32[1,1,32,8192]{3,2,1,0:T(8,128)S(1)}, f32[1,1,32,8192]{3,2,1,0:T(8,128)}, u32[]{:S(2)}) copy-start(f32[1,1,32,8192]{3,2,1,0:T(8,128)} %param.18) | copy-start | bytes 3145732
  0.7 136.0 %copy-start.3 = (f32[1,1,32,8192]{3,2,1,0:T(8,128)S(1)}, f32[1,1,32,8192]{3,2,1,0:T(8,128)}, u32[]{:S(2)}) copy-start(f32[1,1,32,8192]{3,2,1,0:T(8,128)} %param.19) | copy-start | bytes 3145732
  0.7 136.0 %copy-start.4 = (f32[1,1,32,8192]{3,2,1,0:T(8,128)S(1)}, f32[1,1,32,8192]{3,2,1,0:T(8,128)}, u32[]{:S(2)}) copy-start(f32[1,1,32,8192]{3,2,1,0:T(8,128)} %param.20) | copy-start | bytes 3145732
  0.7 136.0 %copy-start.5 = (f32[1,1,32,8192]{3,2,1,0:T(8,128)S(1)}, f32[1,1,32,8192]{3,2,1,0:T(8,128)}, u32[]{:S(2)}) copy-start(f32[1,1,32,8192]{3,2,1,0:T(8,128)} %param.21) | copy-start | bytes 3145732
  0.7 136.0 %copy-start.6 = (f32[1,8192]{1,0:T(1,128)S(1)}, f32[1,8192]{1,0:T(1,128)}, u32[]{:S(2)}) copy-start(f32[1,8192]{1,0:T(1,128)} %gain_ref.1) | copy-start | bytes 98308
